TPU v7x, 512 devices: a whole 4x8x8 slice. The times are simulated.
512 devices in a mesh: section: 8 (over y), dom: 64 (over z, x, core).
Axes of the slice: x: 4, y: 8, z: 8, core: 2. Of those that a mesh axis runs over, the one named last changes fastest.
Arguments:
- node_states: bfloat16 [8, 1, 12288, 512], P('section', None, 'dom'), may hold values from -6 to 6
- edge_features: bfloat16 [1, 24576, 512], P(None, 'dom'), may hold values from -6 to 6
- out_cotangent: bfloat16 [1, 12288, 512], P(None, 'dom'), may hold values from -6 to 6
- edge_weight: bfloat16 [8, 512, 512], P('section'), may hold values from -0.25 to 0.25
- send_weight: bfloat16 [8, 512, 512], P('section'), may hold values from -0.25 to 0.25
- layer_norm_gain: float32 [8, 512], P('section'), may hold values from 0.5 to 1.5
- edge_sender: int32 [24576], P('dom'), may hold values from 0 to 255
- edge_receiver: int32 [24576], P('dom'), may hold values from 0 to 191
- halo_rows: int32 [4096], P('dom'), may hold values from 0 to 191
- block_counts: int32 [64], P('dom'), may hold values from 1 to 3, as said below
Outputs:
- node_grads: bfloat16 [8, 1, 12288, 512], P('section', None, 'dom')
- edge_grads: bfloat16 [1, 24576, 512], P(None, ('dom', 'section'))
- edge_weight_grad: float32 [8, 512, 512], P('section', 'dom')
- send_weight_grad: float32 [8, 512, 512], P('section', 'dom')
- gain_grad: float32 [8, 512], P('section', 'dom')
Inputs may be any that keep to these rules, and one draw needn't show every extreme that they name: `block_counts`: every partition has at least one live block and some partition has all 3 blocks live.
All inputs are finite; a program needn't handle non-finite values.
Results may differ from a plain program's by a relative error of at most 0.028.
Values may be sent and summed in bfloat16 or wider, within the bound.
No kernel may reach another device: no remote copies, remote signals or barrier semaphores. Data moves between devices by JAX's collectives and lax.ppermute only.
A program may use at most 64 MiB of HBM per device.

v0:
```python
import jax
import jax.numpy as jnp
from jax import lax
from jax.sharding import PartitionSpec as P

EDGE_BLOCK = 128


NORM_EPSILON = 1e-05


def padded(block, sides, width):
    for axis, dim in sides:
        count = lax.axis_size(axis)
        forward = [(i, i + 1) for i in range(count - 1)]
        forward.append((count - 1, 0))
        backward = [(target, source) for source, target in forward]
        low = lax.ppermute(
            lax.slice_in_dim(block, block.shape[dim] - width, None, axis=dim), axis, forward
        )
        high = lax.ppermute(lax.slice_in_dim(block, 0, width, axis=dim), axis, backward)
        block = jnp.concatenate([low, block, high], axis=dim)
    return block


def from_behind(value, axis, steps):
    count = lax.axis_size(axis)
    leading, last = (max(0, -steps), min(count, count - steps))
    return lax.ppermute(value, axis, [(source, source + steps) for source in range(leading, last)])


def silu_slope(value):
    sig = jax.nn.sigmoid(value)
    return sig * (1.0 + value * (1.0 - sig))


def onehot_rows(index, count):
    return (index[:, None] == jnp.arange(count, dtype=jnp.int32)[None, :]).astype(jnp.bfloat16)


def on_device(
    node_states,
    edge_features,
    out_cotangent,
    edge_weight,
    send_weight,
    layer_norm_gain,
    edge_sender,
    edge_receiver,
    halo_rows,
    block_counts,
):
    layer_states = node_states[0]
    w_edge = edge_weight[0]
    sender_weight = send_weight[0]
    gain = layer_norm_gain[0]
    sample_draws, nodes, width = layer_states.shape
    edges = edge_features.shape[1]
    rim = halo_rows.shape[0] // 2
    table_rows = nodes + 2 * rim
    blocks = edges // EDGE_BLOCK
    live_blocks = block_counts[0]
    sections = lax.axis_size("section")
    section = lax.axis_index("section")

    def block_parts(block):
        start = block * EDGE_BLOCK
        send_hot = onehot_rows(
            lax.dynamic_slice_in_dim(edge_sender, start, EDGE_BLOCK, 0), table_rows
        )
        recv_hot = onehot_rows(lax.dynamic_slice_in_dim(edge_receiver, start, EDGE_BLOCK, 0), nodes)
        return (start, send_hot, recv_hot)

    def run_blocks(step_fn, init):
        carry = init
        for block in range(blocks):
            carry = step_fn(block, carry, (block < live_blocks).astype(jnp.float32))
        return carry

    projected_features = jnp.dot(
        layer_states, sender_weight, preferred_element_type=jnp.float32
    ).astype(jnp.bfloat16)
    selector_matrix = onehot_rows(halo_rows, nodes)
    outgoing = jnp.einsum(
        "lh,chi->cli", selector_matrix, projected_features, preferred_element_type=jnp.float32
    ).astype(jnp.bfloat16)
    rimmed = padded(outgoing, (("dom", 1),), rim)
    table = jnp.concatenate([projected_features, rimmed[:, :rim], rimmed[:, 3 * rim :]], axis=1)

    def forward_block(block, carry, weight):
        pre_all, agg = carry
        start, send_hot, recv_hot = block_parts(block)
        feats = lax.dynamic_slice_in_dim(edge_features, start, EDGE_BLOCK, 1)
        pre = jnp.dot(feats, w_edge, preferred_element_type=jnp.float32)
        pre = pre + jnp.einsum("et,btd->bed", send_hot, table, preferred_element_type=jnp.float32)
        message = (weight * jax.nn.silu(pre)).astype(jnp.bfloat16)
        agg = agg + jnp.einsum("en,bed->bnd", recv_hot, message, preferred_element_type=jnp.float32)
        pre_all = lax.dynamic_update_slice_in_dim(pre_all, pre, start, 1)
        return (pre_all, agg)

    pre_all, agg = run_blocks(
        forward_block,
        (
            jnp.zeros((sample_draws, edges, width), jnp.float32),
            jnp.zeros((sample_draws, nodes, width), jnp.float32),
        ),
    )
    scale = lax.rsqrt(jnp.mean(agg * agg, axis=-1, keepdims=True) + NORM_EPSILON)
    normed = agg * scale
    micro = 1
    size = sample_draws // micro
    ticks = sections + micro - 1

    def tick(step, carry):
        incoming, grad_edge, grad_send, grad_gain, edge_terms, node_contributions = carry
        index = step - (sections - 1 - section)
        active = (index >= 0) & (index < micro)
        upstream = jnp.where(section == sections - 1, out_cotangent, incoming)
        up_wide = upstream.astype(jnp.float32)

        def part_one():
            pre_slab = pre_all
            dnorm = up_wide * gain
            dagg = (
                scale * (dnorm - normed * jnp.mean(dnorm * normed, axis=-1, keepdims=True))
            ).astype(jnp.bfloat16)
            gain_next = grad_gain + jnp.sum(up_wide * normed, axis=(0, 1))

            def backward_block(block, inner, weight):
                table_grad, edge_acc, slab_terms = inner
                start, send_hot, recv_hot = block_parts(block)
                feats = lax.dynamic_slice_in_dim(edge_features, start, EDGE_BLOCK, 1)
                pre = lax.dynamic_slice_in_dim(pre_slab, start, EDGE_BLOCK, 1)
                gathered = jnp.einsum(
                    "en,bnd->bed", recv_hot, dagg, preferred_element_type=jnp.float32
                )
                dpre = (weight * gathered * silu_slope(pre)).astype(jnp.bfloat16)
                term = jnp.einsum(
                    "bed,fd->bef", dpre, w_edge, preferred_element_type=jnp.float32
                ).astype(jnp.bfloat16)
                slab_terms = lax.dynamic_update_slice_in_dim(slab_terms, term, start, 1)
                edge_acc = edge_acc + jnp.einsum(
                    "bef,bed->fd", feats, dpre, preferred_element_type=jnp.float32
                )
                table_grad = table_grad + jnp.einsum(
                    "et,bed->btd", send_hot, dpre, preferred_element_type=jnp.float32
                )
                return (table_grad, edge_acc, slab_terms)

            start_state = (
                jnp.zeros((size, table_rows, width), jnp.float32),
                grad_edge,
                jnp.zeros((size, edges, width), jnp.bfloat16),
            )
            table_grad, edge_acc, slab_terms = run_blocks(backward_block, start_state)
            return (table_grad, edge_acc, gain_next, slab_terms)

        def spare_one():
            return (
                jnp.zeros((size, table_rows, width), jnp.float32),
                grad_edge,
                grad_gain,
                edge_terms,
            )

        table_grad, grad_edge, grad_gain, edge_terms = lax.cond(active, part_one, spare_one)
        back_out = table_grad[:, nodes:].astype(jnp.bfloat16)
        back_in = padded(back_out, (("dom", 1),), rim)
        backward_rows = jnp.concatenate([back_in[:, :rim], back_in[:, 3 * rim :]], axis=1)

        def part_two():
            returned = jnp.einsum(
                "jg,rju->rgu", selector_matrix, backward_rows, preferred_element_type=jnp.float32
            )
            dproj = (table_grad[:, :nodes] + returned).astype(jnp.bfloat16)
            send_next = grad_send + jnp.einsum(
                "bnf,bnd->fd", layer_states, dproj, preferred_element_type=jnp.float32
            )
            down = (
                up_wide
                + jnp.einsum(
                    "bnd,fd->bnf", dproj, sender_weight, preferred_element_type=jnp.float32
                )
            ).astype(jnp.bfloat16)
            return (down, send_next, down)

        def spare_two():
            return (jnp.zeros((size, nodes, width), jnp.bfloat16), grad_send, node_contributions)

        down, grad_send, node_contributions = lax.cond(active, part_two, spare_two)
        incoming = from_behind(down, "section", -1)
        return (incoming, grad_edge, grad_send, grad_gain, edge_terms, node_contributions)

    init = (
        jnp.zeros((size, nodes, width), jnp.bfloat16),
        jnp.zeros((width, width), jnp.float32),
        jnp.zeros((width, width), jnp.float32),
        jnp.zeros((width,), jnp.float32),
        jnp.zeros((sample_draws, edges, width), jnp.bfloat16),
        jnp.zeros((sample_draws, nodes, width), jnp.bfloat16),
    )
    incoming, grad_edge, grad_send, grad_gain, edge_terms, node_contributions = lax.fori_loop(
        0, ticks, tick, init
    )
    edge_grads = lax.psum_scatter(
        edge_terms.astype(jnp.float32).astype(jnp.bfloat16),
        "section",
        scatter_dimension=1,
        tiled=True,
    )
    edge_part, send_part, gain_part = (
        lax.psum_scatter(grad_edge[None], "dom", scatter_dimension=1, tiled=True),
        lax.psum_scatter(grad_send[None], "dom", scatter_dimension=1, tiled=True),
        lax.psum_scatter(grad_gain[None], "dom", scatter_dimension=1, tiled=True),
    )
    return (node_contributions[None], edge_grads, edge_part, send_part, gain_part)


def solution(mesh):
    return jax.shard_map(
        on_device,
        mesh=mesh,
        in_specs=(
            P("section", None, "dom", None),
            P(None, "dom", None),
            P(None, "dom", None),
            P("section", None, None),
            P("section", None, None),
            P("section", None),
            P("dom"),
            P("dom"),
            P("dom"),
            P("dom"),
        ),
        out_specs=(
            P("section", None, "dom", None),
            P(None, ("dom", "section"), None),
            P("section", "dom", None),
            P("section", "dom", None),
            P("section", "dom"),
        ),
        check_vma=False,
    )
```

profile of v0, /device:TPU:1, one launch (start us, length us, event | category | flops | bytes accessed | tf_op | source)
XLA Modules:
  0.0 595.6 jit_solution(17291581331069117592)
XLA Ops:
  9.8 4.5 collective-permute-start.3
  14.3 6.2 %collective-permute-start.4 = (bf16[1,32,512]{2,1,0:T(8,128)(2,1)S(1)}, bf16[1,32,512]{2,1,0:T(8,128)(2,1)S(1)}, u32[]{:S(2)}, u32[]{:S(2)}) collective-permute-start(bf16[1,32,512]{2,1,0:T(8,128)(2,1)S(1)} %get-tuple-element.754), channel_id=1, source_target_pairs={{1,0},{2,1},{3,2},{4,3},{5,4},{6,5},{7,6},{8,7},{9,8},{10,9},{11,1... | collective-permute-start | bytes 98312 | tf_op jit(solution)/shard_map/ppermute | solution.py:21
  30.4 355.8 %while.26 = (s32[]{:T(128)}, bf16[1,192,512]{2,1,0:T(8,128)(2,1)S(1)}, f32[512,512]{0,1:T(8,128)S(1)}, f32[512,512]{0,1:T(8,128)}, f32[512]{0:T(512)S(1)}, /*ind...) while((s32[]{:T(128)}, ...), condition=%wide.region_8.9_spmd.clone, body=%wide.region_1.8_spmd.clone.sunk | while | flops 798097408 | bytes 45033292 | solution.py:202
  32.1 7.2 %collective-permute-start = (bf16[1,32,512]{2,1,0:T(8,128)(2,1)S(1)}, bf16[1,32,512]{2,1,0:T(8,128)(2,1)S(1)}, u32[]{:S(2)}, u32[]{:S(2)}) collective-permute-start(bf16[1,32,512]{2,1,0:T(8,128)(2,1)S(1)} %get-tuple-element.912), channel_id=1, source_target_pairs={{1,0},{2,1},{3,2},{4,3},{5,4},{6,5},{7,6},{8,7},{9,8},{10,9},{11,1... | collective-permute-start | bytes 98312 | tf_op jit(solution)/shard_map/while/body/eval_jaxpr/ppermute | solution.py:21
  42.6 3.3 collective-permute-done.1
  48.6 5.3 collective-permute-done.2
  55.6 9.0 %collective-permute-start = (bf16[1,32,512]{2,1,0:T(8,128)(2,1)S(1)}, bf16[1,32,512]{2,1,0:T(8,128)(2,1)S(1)}, u32[]{:S(2)}, u32[]{:S(2)}) collective-permute-start(bf16[1,32,512]{2,1,0:T(8,128)(2,1)S(1)} %get-tuple-element.912), channel_id=1, source_target_pairs={{1,0},{2,1},{3,2},{4,3},{5,4},{6,5},{7,6},{8,7},{9,8},{10,9},{11,1... | collective-permute-start | bytes 98312 | tf_op jit(solution)/shard_map/while/body/eval_jaxpr/ppermute | solution.py:21
  70.5 5.3 collective-permute-done.2
  77.6 8.3 %collective-permute-start = (bf16[1,32,512]{2,1,0:T(8,128)(2,1)S(1)}, bf16[1,32,512]{2,1,0:T(8,128)(2,1)S(1)}, u32[]{:S(2)}, u32[]{:S(2)}) collective-permute-start(bf16[1,32,512]{2,1,0:T(8,128)(2,1)S(1)} %get-tuple-element.912), channel_id=1, source_target_pairs={{1,0},{2,1},{3,2},{4,3},{5,4},{6,5},{7,6},{8,7},{9,8},{10,9},{11,1... | collective-permute-start | bytes 98312 | tf_op jit(solution)/shard_map/while/body/eval_jaxpr/ppermute | solution.py:21
  91.8 5.3 collective-permute-done.2
  98.9 8.3 %collective-permute-start = (bf16[1,32,512]{2,1,0:T(8,128)(2,1)S(1)}, bf16[1,32,512]{2,1,0:T(8,128)(2,1)S(1)}, u32[]{:S(2)}, u32[]{:S(2)}) collective-permute-start(bf16[1,32,512]{2,1,0:T(8,128)(2,1)S(1)} %get-tuple-element.912), channel_id=1, source_target_pairs={{1,0},{2,1},{3,2},{4,3},{5,4},{6,5},{7,6},{8,7},{9,8},{10,9},{11,1... | collective-permute-start | bytes 98312 | tf_op jit(solution)/shard_map/while/body/eval_jaxpr/ppermute | solution.py:21
  113.1 5.5 collective-permute-done.2
  120.4 8.1 %collective-permute-start = (bf16[1,32,512]{2,1,0:T(8,128)(2,1)S(1)}, bf16[1,32,512]{2,1,0:T(8,128)(2,1)S(1)}, u32[]{:S(2)}, u32[]{:S(2)}) collective-permute-start(bf16[1,32,512]{2,1,0:T(8,128)(2,1)S(1)} %get-tuple-element.912), channel_id=1, source_target_pairs={{1,0},{2,1},{3,2},{4,3},{5,4},{6,5},{7,6},{8,7},{9,8},{10,9},{11,1... | collective-permute-start | bytes 98312 | tf_op jit(solution)/shard_map/while/body/eval_jaxpr/ppermute | solution.py:21
  134.4 6.7 %collective-permute-done.2 = bf16[1,192,512]{2,1,0:T(8,128)(2,1)S(1)} collective-permute-done((bf16[1,192,512]{2,1,0:T(8,128)(2,1)}, bf16[1,192,512]{2,1,0:T(8,128)(2,1)S(1)}, u32[]{:S(2)}, u32[]{:S(2)}) %collective-permute-start.2) | collective-permute-done | bytes 196640 | tf_op jit(solution)/shard_map/while/body/eval_jaxpr/ppermute | solution.py:29
  142.9 8.0 %collective-permute-start = (bf16[1,32,512]{2,1,0:T(8,128)(2,1)S(1)}, bf16[1,32,512]{2,1,0:T(8,128)(2,1)S(1)}, u32[]{:S(2)}, u32[]{:S(2)}) collective-permute-start(bf16[1,32,512]{2,1,0:T(8,128)(2,1)S(1)} %get-tuple-element.912), channel_id=1, source_target_pairs={{1,0},{2,1},{3,2},{4,3},{5,4},{6,5},{7,6},{8,7},{9,8},{10,9},{11,1... | collective-permute-start | bytes 98312 | tf_op jit(solution)/shard_map/while/body/eval_jaxpr/ppermute | solution.py:21
  156.8 6.8 %collective-permute-done.2 = bf16[1,192,512]{2,1,0:T(8,128)(2,1)S(1)} collective-permute-done((bf16[1,192,512]{2,1,0:T(8,128)(2,1)}, bf16[1,192,512]{2,1,0:T(8,128)(2,1)S(1)}, u32[]{:S(2)}, u32[]{:S(2)}) %collective-permute-start.2) | collective-permute-done | bytes 196640 | tf_op jit(solution)/shard_map/while/body/eval_jaxpr/ppermute | solution.py:29
  165.4 8.0 %collective-permute-start = (bf16[1,32,512]{2,1,0:T(8,128)(2,1)S(1)}, bf16[1,32,512]{2,1,0:T(8,128)(2,1)S(1)}, u32[]{:S(2)}, u32[]{:S(2)}) collective-permute-start(bf16[1,32,512]{2,1,0:T(8,128)(2,1)S(1)} %get-tuple-element.912), channel_id=1, source_target_pairs={{1,0},{2,1},{3,2},{4,3},{5,4},{6,5},{7,6},{8,7},{9,8},{10,9},{11,1... | collective-permute-start | bytes 98312 | tf_op jit(solution)/shard_map/while/body/eval_jaxpr/ppermute | solution.py:21
  179.4 162.4 %collective-permute-done.2 = bf16[1,192,512]{2,1,0:T(8,128)(2,1)S(1)} collective-permute-done((bf16[1,192,512]{2,1,0:T(8,128)(2,1)}, bf16[1,192,512]{2,1,0:T(8,128)(2,1)S(1)}, u32[]{:S(2)}, u32[]{:S(2)}) %collective-permute-start.2) | collective-permute-done | bytes 196640 | tf_op jit(solution)/shard_map/while/body/eval_jaxpr/ppermute | solution.py:29
  341.8 18.7 %conditional.6 = (f32[1,256,512]{1,2,0:T(8,128)S(1)}, f32[512,512]{0,1:T(8,128)S(1)}, f32[512]{0:T(512)S(1)}, bf16[1,384,512]{2,1,0:T(8,128)(2,1)}) conditional(s32[]{:T(128)} %convert_element_type.193, (f32[512,512]{0,1:T(8,128)S(1)}, f32[512]{0:T(512)S(1)}, bf16[1,384,512]{2,1,0:T(8,128)(2,1)}) %tuple.91, (s32[]{:T(128)}, ...), branch_computations={%region_2.2_spmd, %region_3.5_spmd} | conditional | flops 583180288 | bytes 24929168 | solution.py:166
  362.2 8.1 %collective-permute-start = (bf16[1,32,512]{2,1,0:T(8,128)(2,1)S(1)}, bf16[1,32,512]{2,1,0:T(8,128)(2,1)S(1)}, u32[]{:S(2)}, u32[]{:S(2)}) collective-permute-start(bf16[1,32,512]{2,1,0:T(8,128)(2,1)S(1)} %get-tuple-element.912), channel_id=1, source_target_pairs={{1,0},{2,1},{3,2},{4,3},{5,4},{6,5},{7,6},{8,7},{9,8},{10,9},{11,1... | collective-permute-start | bytes 98312 | tf_op jit(solution)/shard_map/while/body/eval_jaxpr/ppermute | solution.py:21
  374.1 5.4 conditional.7
  380.8 5.3 collective-permute-done.2
  391.3 129.9 %all-reduce.4 = f32[1,512]{1,0:T(1,128)S(1)} all-reduce(f32[1,512]{1,0:T(1,128)S(1)} %bitcast.226), channel_id=5, replica_groups=mesh['section'=8,'dom'=64] {'dom'}, use_global_device_ids=true, to_apply=%region_12.13.clone | all-reduce | flops 512 | bytes 4096
  521.9 64.9 %all-reduce.8.cloned.1.call-done = (f32[1,512,512]{2,1,0:T(8,128)}, f32[1,512,512]{2,1,0:T(8,128)}) async-done(((f32[1,512,512]{2,1,0:T(8,128)}, f32[1,512,512]{2,1,0:T(8,128)}), (f32[1,512,512]{2,1,0:T(8,128)}, f32[1,512,512]{2,1,0:T(8,128)})) %all-reduce.8.cloned.1.call-update) | async-done | bytes 2097168
  (210 shorter events, 104.4 us)
Async XLA Ops:
  8.0 578.8 %all-reduce.8.cloned.1.call-start = ((), (), s32[]{:S(2)}) async-start(), calls=%async_computation.2 | async-start | bytes 4194304
  9.8 13.4 %collective-permute-start.3 = (bf16[1,32,512]{2,1,0:T(8,128)(2,1)S(1)}, bf16[1,32,512]{2,1,0:T(8,128)(2,1)S(1)}, u32[]{:S(2)}, u32[]{:S(2)}) collective-permute-start(bf16[1,32,512]{2,1,0:T(8,128)(2,1)S(1)} %get-tuple-element.753), channel_id=1, source_target_pairs={{0,1},{1,2},{2,3},{3,4},{4,5},{5,6},{6,7},{7,8},{8,9},{9,10},{10,1... | collective-permute-start | bytes 98312 | tf_op jit(solution)/shard_map/ppermute | solution.py:18
  14.3 8.9 %collective-permute-start.4 = (bf16[1,32,512]{2,1,0:T(8,128)(2,1)S(1)}, bf16[1,32,512]{2,1,0:T(8,128)(2,1)S(1)}, u32[]{:S(2)}, u32[]{:S(2)}) collective-permute-start(bf16[1,32,512]{2,1,0:T(8,128)(2,1)S(1)} %get-tuple-element.754), channel_id=1, source_target_pairs={{1,0},{2,1},{3,2},{4,3},{5,4},{6,5},{7,6},{8,7},{9,8},{10,9},{11,1... | collective-permute-start | bytes 98312 | tf_op jit(solution)/shard_map/ppermute | solution.py:21
  32.1 10.5 %collective-permute-start = (bf16[1,32,512]{2,1,0:T(8,128)(2,1)S(1)}, bf16[1,32,512]{2,1,0:T(8,128)(2,1)S(1)}, u32[]{:S(2)}, u32[]{:S(2)}) collective-permute-start(bf16[1,32,512]{2,1,0:T(8,128)(2,1)S(1)} %get-tuple-element.912), channel_id=1, source_target_pairs={{1,0},{2,1},{3,2},{4,3},{5,4},{6,5},{7,6},{8,7},{9,8},{10,9},{11,1... | collective-permute-start | bytes 98312 | tf_op jit(solution)/shard_map/while/body/eval_jaxpr/ppermute | solution.py:21
  39.4 6.6 %collective-permute-start.1 = (bf16[1,32,512]{2,1,0:T(8,128)(2,1)S(1)}, bf16[1,32,512]{2,1,0:T(8,128)(2,1)S(1)}, u32[]{:S(2)}, u32[]{:S(2)}) collective-permute-start(bf16[1,32,512]{2,1,0:T(8,128)(2,1)S(1)} %get-tuple-element.913), channel_id=1, source_target_pairs={{0,1},{1,2},{2,3},{3,4},{4,5},{5,6},{6,7},{7,8},{8,9},{9,10},{10,1... | collective-permute-start | bytes 98312 | tf_op jit(solution)/shard_map/while/body/eval_jaxpr/ppermute | solution.py:18
  47.3 6.6 %collective-permute-start.2 = (bf16[1,192,512]{2,1,0:T(8,128)(2,1)}, bf16[1,192,512]{2,1,0:T(8,128)(2,1)S(1)}, u32[]{:S(2)}, u32[]{:S(2)}) collective-permute-start(bf16[1,192,512]{2,1,0:T(8,128)(2,1)} %get-tuple-element.914), channel_id=1, source_target_pairs={{64,0},{128,64},{192,128},{256,192},{320,256},{384,320},{448,384},... | collective-permute-start | bytes 589832 | tf_op jit(solution)/shard_map/while/body/eval_jaxpr/ppermute | solution.py:29
  55.6 12.3 %collective-permute-start = (bf16[1,32,512]{2,1,0:T(8,128)(2,1)S(1)}, bf16[1,32,512]{2,1,0:T(8,128)(2,1)S(1)}, u32[]{:S(2)}, u32[]{:S(2)}) collective-permute-start(bf16[1,32,512]{2,1,0:T(8,128)(2,1)S(1)} %get-tuple-element.912), channel_id=1, source_target_pairs={{1,0},{2,1},{3,2},{4,3},{5,4},{6,5},{7,6},{8,7},{9,8},{10,9},{11,1... | collective-permute-start | bytes 98312 | tf_op jit(solution)/shard_map/while/body/eval_jaxpr/ppermute | solution.py:21
  64.6 3.3 collective-permute-start.1
  69.2 6.6 %collective-permute-start.2 = (bf16[1,192,512]{2,1,0:T(8,128)(2,1)}, bf16[1,192,512]{2,1,0:T(8,128)(2,1)S(1)}, u32[]{:S(2)}, u32[]{:S(2)}) collective-permute-start(bf16[1,192,512]{2,1,0:T(8,128)(2,1)} %get-tuple-element.914), channel_id=1, source_target_pairs={{64,0},{128,64},{192,128},{256,192},{320,256},{384,320},{448,384},... | collective-permute-start | bytes 589832 | tf_op jit(solution)/shard_map/while/body/eval_jaxpr/ppermute | solution.py:29
  77.6 11.6 %collective-permute-start = (bf16[1,32,512]{2,1,0:T(8,128)(2,1)S(1)}, bf16[1,32,512]{2,1,0:T(8,128)(2,1)S(1)}, u32[]{:S(2)}, u32[]{:S(2)}) collective-permute-start(bf16[1,32,512]{2,1,0:T(8,128)(2,1)S(1)} %get-tuple-element.912), channel_id=1, source_target_pairs={{1,0},{2,1},{3,2},{4,3},{5,4},{6,5},{7,6},{8,7},{9,8},{10,9},{11,1... | collective-permute-start | bytes 98312 | tf_op jit(solution)/shard_map/while/body/eval_jaxpr/ppermute | solution.py:21
  85.9 3.3 collective-permute-start.1
  90.5 6.6 %collective-permute-start.2 = (bf16[1,192,512]{2,1,0:T(8,128)(2,1)}, bf16[1,192,512]{2,1,0:T(8,128)(2,1)S(1)}, u32[]{:S(2)}, u32[]{:S(2)}) collective-permute-start(bf16[1,192,512]{2,1,0:T(8,128)(2,1)} %get-tuple-element.914), channel_id=1, source_target_pairs={{64,0},{128,64},{192,128},{256,192},{320,256},{384,320},{448,384},... | collective-permute-start | bytes 589832 | tf_op jit(solution)/shard_map/while/body/eval_jaxpr/ppermute | solution.py:29
  98.9 11.6 %collective-permute-start = (bf16[1,32,512]{2,1,0:T(8,128)(2,1)S(1)}, bf16[1,32,512]{2,1,0:T(8,128)(2,1)S(1)}, u32[]{:S(2)}, u32[]{:S(2)}) collective-permute-start(bf16[1,32,512]{2,1,0:T(8,128)(2,1)S(1)} %get-tuple-element.912), channel_id=1, source_target_pairs={{1,0},{2,1},{3,2},{4,3},{5,4},{6,5},{7,6},{8,7},{9,8},{10,9},{11,1... | collective-permute-start | bytes 98312 | tf_op jit(solution)/shard_map/while/body/eval_jaxpr/ppermute | solution.py:21
  107.2 3.3 collective-permute-start.1
  111.8 6.8 %collective-permute-start.2 = (bf16[1,192,512]{2,1,0:T(8,128)(2,1)}, bf16[1,192,512]{2,1,0:T(8,128)(2,1)S(1)}, u32[]{:S(2)}, u32[]{:S(2)}) collective-permute-start(bf16[1,192,512]{2,1,0:T(8,128)(2,1)} %get-tuple-element.914), channel_id=1, source_target_pairs={{64,0},{128,64},{192,128},{256,192},{320,256},{384,320},{448,384},... | collective-permute-start | bytes 589832 | tf_op jit(solution)/shard_map/while/body/eval_jaxpr/ppermute | solution.py:29
  120.4 11.4 %collective-permute-start = (bf16[1,32,512]{2,1,0:T(8,128)(2,1)S(1)}, bf16[1,32,512]{2,1,0:T(8,128)(2,1)S(1)}, u32[]{:S(2)}, u32[]{:S(2)}) collective-permute-start(bf16[1,32,512]{2,1,0:T(8,128)(2,1)S(1)} %get-tuple-element.912), channel_id=1, source_target_pairs={{1,0},{2,1},{3,2},{4,3},{5,4},{6,5},{7,6},{8,7},{9,8},{10,9},{11,1... | collective-permute-start | bytes 98312 | tf_op jit(solution)/shard_map/while/body/eval_jaxpr/ppermute | solution.py:21
  133.1 8.0 %collective-permute-start.2 = (bf16[1,192,512]{2,1,0:T(8,128)(2,1)}, bf16[1,192,512]{2,1,0:T(8,128)(2,1)S(1)}, u32[]{:S(2)}, u32[]{:S(2)}) collective-permute-start(bf16[1,192,512]{2,1,0:T(8,128)(2,1)} %get-tuple-element.914), channel_id=1, source_target_pairs={{64,0},{128,64},{192,128},{256,192},{320,256},{384,320},{448,384},... | collective-permute-start | bytes 589832 | tf_op jit(solution)/shard_map/while/body/eval_jaxpr/ppermute | solution.py:29
  142.9 11.3 %collective-permute-start = (bf16[1,32,512]{2,1,0:T(8,128)(2,1)S(1)}, bf16[1,32,512]{2,1,0:T(8,128)(2,1)S(1)}, u32[]{:S(2)}, u32[]{:S(2)}) collective-permute-start(bf16[1,32,512]{2,1,0:T(8,128)(2,1)S(1)} %get-tuple-element.912), channel_id=1, source_target_pairs={{1,0},{2,1},{3,2},{4,3},{5,4},{6,5},{7,6},{8,7},{9,8},{10,9},{11,1... | collective-permute-start | bytes 98312 | tf_op jit(solution)/shard_map/while/body/eval_jaxpr/ppermute | solution.py:21
  155.6 8.1 %collective-permute-start.2 = (bf16[1,192,512]{2,1,0:T(8,128)(2,1)}, bf16[1,192,512]{2,1,0:T(8,128)(2,1)S(1)}, u32[]{:S(2)}, u32[]{:S(2)}) collective-permute-start(bf16[1,192,512]{2,1,0:T(8,128)(2,1)} %get-tuple-element.914), channel_id=1, source_target_pairs={{64,0},{128,64},{192,128},{256,192},{320,256},{384,320},{448,384},... | collective-permute-start | bytes 589832 | tf_op jit(solution)/shard_map/while/body/eval_jaxpr/ppermute | solution.py:29
  165.4 11.3 %collective-permute-start = (bf16[1,32,512]{2,1,0:T(8,128)(2,1)S(1)}, bf16[1,32,512]{2,1,0:T(8,128)(2,1)S(1)}, u32[]{:S(2)}, u32[]{:S(2)}) collective-permute-start(bf16[1,32,512]{2,1,0:T(8,128)(2,1)S(1)} %get-tuple-element.912), channel_id=1, source_target_pairs={{1,0},{2,1},{3,2},{4,3},{5,4},{6,5},{7,6},{8,7},{9,8},{10,9},{11,1... | collective-permute-start | bytes 98312 | tf_op jit(solution)/shard_map/while/body/eval_jaxpr/ppermute | solution.py:21
  178.1 163.7 %collective-permute-start.2 = (bf16[1,192,512]{2,1,0:T(8,128)(2,1)}, bf16[1,192,512]{2,1,0:T(8,128)(2,1)S(1)}, u32[]{:S(2)}, u32[]{:S(2)}) collective-permute-start(bf16[1,192,512]{2,1,0:T(8,128)(2,1)} %get-tuple-element.914), channel_id=1, source_target_pairs={{64,0},{128,64},{192,128},{256,192},{320,256},{384,320},{448,384},... | collective-permute-start | bytes 589832 | tf_op jit(solution)/shard_map/while/body/eval_jaxpr/ppermute | solution.py:29
  362.2 11.3 %collective-permute-start = (bf16[1,32,512]{2,1,0:T(8,128)(2,1)S(1)}, bf16[1,32,512]{2,1,0:T(8,128)(2,1)S(1)}, u32[]{:S(2)}, u32[]{:S(2)}) collective-permute-start(bf16[1,32,512]{2,1,0:T(8,128)(2,1)S(1)} %get-tuple-element.912), channel_id=1, source_target_pairs={{1,0},{2,1},{3,2},{4,3},{5,4},{6,5},{7,6},{8,7},{9,8},{10,9},{11,1... | collective-permute-start | bytes 98312 | tf_op jit(solution)/shard_map/while/body/eval_jaxpr/ppermute | solution.py:21
  379.5 6.6 %collective-permute-start.2 = (bf16[1,192,512]{2,1,0:T(8,128)(2,1)}, bf16[1,192,512]{2,1,0:T(8,128)(2,1)S(1)}, u32[]{:S(2)}, u32[]{:S(2)}) collective-permute-start(bf16[1,192,512]{2,1,0:T(8,128)(2,1)} %get-tuple-element.914), channel_id=1, source_target_pairs={{64,0},{128,64},{192,128},{256,192},{320,256},{384,320},{448,384},... | collective-permute-start | bytes 589832 | tf_op jit(solution)/shard_map/while/body/eval_jaxpr/ppermute | solution.py:29
  388.8 199.3 %reduce-scatter.5.cloned.1.call-start = ((), (), s32[]{:S(2)}) async-start(), calls=%async_computation.1 | async-start | bytes 442368 | tf_op jit(solution)/shard_map/reduce_scatter | solution.py:205
  (30 other events, 376.4 us)
Sparse Core Ops, SparseCore 0:
  389.0 197.7 all-reduce.7
Sparse Core Ops, SparseCore 1:
  392.7 32.3 reduce-scatter.4
where the time goes:
time: 598 us; the launch traced here: 596 us
  waiting for transfers between devices  272 us (45%)
  blocking collectives  130 us (22%)
  starting transfers between devices  102 us (17%)
  local copies, waits for them, and re-layouts  34.6 us (6%)
  other arithmetic  19.6 us (3%)
  matrix products  18.6 us (3%)
  between operations  17 us (3%)
    ppermute x8, waiting for transfers between devices, from_behind(): lax.ppermute(value, axis, [(source, source + steps) for source in range(l...  203 us
    unnamed x1, blocking collectives  130 us
    ppermute x9, starting transfers between devices, padded(): lax.ppermute(lax.slice_in_dim(block, 0, width, axis=dim), axis, backward)  71.3 us
    unnamed x3, waiting for transfers between devices  65.4 us
    ppermute x9, starting transfers between devices, padded(): lax.ppermute(lax.slice_in_dim(block, block.shape[dim] - width, None, axis...  19.9 us
  transfers between devices with their start and end apart: 28, of which 10 were waited for; matrix products, arithmetic and copies ran while one was open for 3% of the time, Pallas kernels for 0%

commit v1 on v0

v1 whole, which is shorter than its diff:
```python
import numpy as np
import jax
import jax.numpy as jnp
from jax import lax
from jax.sharding import PartitionSpec as P

EDGE_BLOCK = 128
NORM_EPSILON = 1e-05

GRAY = {2: (0, 1), 4: (0, 1, 3, 2), 8: (0, 1, 3, 2, 6, 7, 5, 4)}

STEPS = {
    0: (("c", 0), ("x", 0), ("z", 0), ("x", 1), ("z", 1), ("z", 2)),
    1: (("c", 0), ("z", 0), ("x", 0), ("z", 1), ("x", 1), ("z", 2)),
}


def coordinates(p):
    return {"z": p // 8, "x": (p // 2) % 4, "c": p % 2}


def index_of(at):
    return at["z"] * 8 + at["x"] * 2 + at["c"]


SIZES = {"z": 8, "x": 4, "c": 2}


def flipped(p, step):
    axis, bit = step
    at = dict(coordinates(p))
    gray = GRAY[SIZES[axis]]
    at[axis] = gray.index(gray[at[axis]] ^ (1 << bit))
    return index_of(at)


def dom_partner(p, k):
    return flipped(p, STEPS[p % 2][k])


def dom_order():
    table = np.zeros((64, 64), np.int32)
    for p in range(64):
        for j in range(64):
            q = p
            core = (p % 2) ^ (j >> 5)
            for k in range(6):
                if (j >> (5 - k)) & 1:
                    q = flipped(q, STEPS[core][k])
            table[p, j] = q
    return table


def section_flip(s, bit):
    gray = GRAY[8]
    return gray.index(gray[s] ^ (1 << bit))


def section_order():
    table = np.zeros((8, 8), np.int32)
    for s in range(8):
        for j in range(8):
            q = s
            for k in range(3):
                if (j >> (2 - k)) & 1:
                    q = section_flip(q, k)
            table[s, j] = q
    return table


def onehot(index, count):
    return (index[:, None] == jnp.arange(count, dtype=jnp.int32)[None, :]).astype(jnp.bfloat16)


def onehot_t(index, count):
    return (jnp.arange(count, dtype=jnp.int32)[:, None] == index[None, :]).astype(jnp.bfloat16)


def dot(a, b):
    return jnp.dot(a, b, preferred_element_type=jnp.float32)


def dot_t(a, b):
    return lax.dot_general(a, b, (((1,), (1,)), ((), ())), preferred_element_type=jnp.float32)


def spread(chunks, size):
    return (chunks[:, None] * size + jnp.arange(size, dtype=jnp.int32)[None, :]).reshape(-1)


def on_device(
    node_states,
    edge_features,
    out_cotangent,
    edge_weight,
    send_weight,
    layer_norm_gain,
    edge_sender,
    edge_receiver,
    halo_rows,
    block_counts,
):
    bf16, f32 = jnp.bfloat16, jnp.float32
    h = node_states[0, 0]
    feats = edge_features[0]
    w_edge, w_send, gain = edge_weight[0], send_weight[0], layer_norm_gain[0]
    nodes, width = h.shape
    edges = feats.shape[0]
    rim = halo_rows.shape[0] // 2
    rows = nodes + 2 * rim
    sections, doms = lax.axis_size("section"), lax.axis_size("dom")
    section, dom = lax.axis_index("section"), lax.axis_index("dom")

    up_pairs = [(p, (p + 1) % doms) for p in range(doms)]
    down_pairs = [(p, (p - 1) % doms) for p in range(doms)]

    select = onehot(halo_rows, nodes)
    select_t = onehot_t(halo_rows, nodes)
    chosen = dot(select, h).astype(bf16)
    from_low = lax.ppermute(chosen[rim:], "dom", up_pairs)
    from_high = lax.ppermute(chosen[:rim], "dom", down_pairs)
    h_rim = jnp.concatenate([from_low, from_high], axis=0)
    send_hot = onehot(edge_sender, rows)
    send_hot_t = onehot_t(edge_sender, rows)
    recv_hot = onehot(edge_receiver, nodes)
    recv_hot_t = onehot_t(edge_receiver, nodes)
    live = (jnp.arange(edges, dtype=jnp.int32) // EDGE_BLOCK < block_counts[0]).astype(f32)[:, None]
    own = dot(h, w_send).astype(bf16)
    pre = dot(feats, w_edge) + dot(send_hot[:, :nodes], own)
    pre = pre + dot(send_hot[:, nodes:], dot(h_rim, w_send).astype(bf16))
    sig = jax.nn.sigmoid(pre)
    message = (live * (pre * sig)).astype(bf16)
    slope = live * (sig * (1.0 + pre * (1.0 - sig)))
    agg = dot(recv_hot_t, message)
    scale = lax.rsqrt(jnp.mean(agg * agg, axis=-1, keepdims=True) + NORM_EPSILON)
    normed = agg * scale

    def backward(up):
        up_wide = up.astype(f32)
        dnorm = up_wide * gain
        dagg = scale * (dnorm - normed * jnp.mean(dnorm * normed, axis=-1, keepdims=True))
        gathered = dot(recv_hot, dagg.astype(bf16))
        dpre = (slope * gathered).astype(bf16)
        return dpre, dot(send_hot_t, dpre).astype(bf16)

    def parts(up, table):
        back = dot_t(table, w_send)
        return (up.astype(f32) + back[:nodes]).astype(bf16), back[nodes:].astype(bf16)

    def joined(part, rims):
        return (part.astype(f32) + dot(select_t, rims)).astype(bf16)

    def hop(value, t, shift):
        top = sections - 1 - t
        pairs = [(top * doms + p, (top - 1) * doms + (p + shift) % doms) for p in range(doms)]
        return lax.ppermute(value, ("section", "dom"), pairs)

    up = out_cotangent[0]
    held = jnp.where(section == sections - 1, up, jnp.zeros_like(up))
    held_rims = jnp.zeros((2 * rim, width), bf16)
    for t in range(sections - 1):
        _, table = backward(up)
        part, edge_rows = parts(up, table)
        part = hop(part, t, 0)
        rims = jnp.concatenate([hop(edge_rows[rim:], t, 1), hop(edge_rows[:rim], t, -1)], axis=0)
        up = joined(part, rims)
        if t < sections - 2:
            held, held_rims = held + part, held_rims + rims

    held, held_rims = lax.optimization_barrier((held, held_rims))
    up = joined(held + part, held_rims + rims)

    order = lax.dynamic_index_in_dim(jnp.asarray(dom_order()), dom, 0, keepdims=False)
    mixer = onehot(spread(order, width // doms), width)
    feats_t = dot_t(mixer, feats).astype(bf16)
    h_t = jnp.concatenate([dot_t(mixer, h), dot_t(mixer, h_rim)], axis=1).astype(bf16)
    half = width // 2

    dpre, table = backward(up)
    gain_part = jnp.sum(up.astype(f32) * normed, axis=0)

    def gain_rows(total):
        high = total.astype(bf16)
        low = (total - high.astype(f32)).astype(bf16)
        return jnp.concatenate([high[None], low[None], jnp.zeros((6, width), bf16)], axis=0)

    edge_keep, send_keep = dot(feats_t[:half], dpre), dot(h_t[:half], table)
    edge_send, send_send = dot(feats_t[half:], dpre), dot(h_t[half:], table)
    keep = jnp.concatenate([edge_keep, send_keep], axis=0)
    away = jnp.concatenate([edge_send, send_send], axis=0).astype(bf16)
    total = gain_part
    size = half
    for k in range(6):
        pairs = [(p, dom_partner(p, k)) for p in range(doms)]
        got = lax.ppermute(jnp.concatenate([away, gain_rows(total)], axis=0), "dom", pairs)
        keep = keep + got[: 2 * size].astype(f32)
        total = total + got[2 * size].astype(f32) + got[2 * size + 1].astype(f32)
        if k < 5:
            size = size // 2
            away = jnp.concatenate([keep[size : 2 * size], keep[3 * size :]], axis=0).astype(bf16)
            keep = jnp.concatenate([keep[:size], keep[2 * size : 3 * size]], axis=0)
    edge_grad, send_grad = keep[:size], keep[size:]
    gain_grad = lax.dynamic_slice_in_dim(total, dom * size, size, 0)

    part, edge_rows = parts(up, table)
    rims = jnp.concatenate(
        [
            lax.ppermute(edge_rows[rim:], "dom", up_pairs),
            lax.ppermute(edge_rows[:rim], "dom", down_pairs),
        ],
        axis=0,
    )
    node_grads = joined(part, rims)

    s_order = lax.dynamic_index_in_dim(jnp.asarray(section_order()), section, 0, keepdims=False)
    s_mixer = onehot(spread(s_order, edges // sections), edges)
    term = dot_t(dot(s_mixer, dpre).astype(bf16), w_edge).astype(bf16)
    for k in range(3):
        pairs = [(s, section_flip(s, k)) for s in range(sections)]
        middle = term.shape[0] // 2
        got = lax.ppermute(term[middle:], "section", pairs)
        term = (term[:middle].astype(f32) + got.astype(f32)).astype(bf16)

    return (
        node_grads[None, None],
        term[None],
        edge_grad[None],
        send_grad[None],
        gain_grad[None],
    )


def solution(mesh):
    return jax.shard_map(
        on_device,
        mesh=mesh,
        in_specs=(
            P("section", None, "dom", None),
            P(None, "dom", None),
            P(None, "dom", None),
            P("section", None, None),
            P("section", None, None),
            P("section", None),
            P("dom"),
            P("dom"),
            P("dom"),
            P("dom"),
        ),
        out_specs=(
            P("section", None, "dom", None),
            P(None, ("dom", "section"), None),
            P("section", "dom", None),
            P("section", "dom", None),
            P("section", "dom"),
        ),
        check_vma=False,
    )
```

time: 598 us -> 191 us (0.32)
  the two profiles are of different devices: /device:TPU:1 before, /device:TPU:6 now
where the time goes in v1:
time: 191 us; the launch traced here: 190 us
  waiting for transfers between devices  81.9 us (43%)
  starting transfers between devices  61.4 us (32%)
  matrix products  23.9 us (13%)
  local copies, waits for them, and re-layouts  13.9 us (7%)
  other arithmetic  6.04 us (3%)
  between operations  2.74 us (1%)
    ppermute x21, waiting for transfers between devices, hop(): return lax.ppermute(value, ('section', 'dom'), pairs)  53.1 us
    ppermute x6, starting transfers between devices, on_device(): lax.ppermute(jnp.concatenate([away, gain_rows(total)], axis=0), 'dom', pa...  29.3 us
    ppermute x6, waiting for transfers between devices, on_device(): lax.ppermute(jnp.concatenate([away, gain_rows(total)], axis=0), 'dom', pa...  17.7 us
    ppermute x21, starting transfers between devices, hop(): return lax.ppermute(value, ('section', 'dom'), pairs)  16.3 us
    dot_general x26, matrix products, dot(): return jnp.dot(a, b, preferred_element_type=jnp.float32)  15.3 us
    ppermute x3, waiting for transfers between devices, on_device(): got = lax.ppermute(term[middle:], 'section', pairs)  11.1 us
    dot_general x12, matrix products, dot_t(): lax.dot_general(a, b, (((1,), (1,)), ((), ())), preferred_element_type=jn...  8.59 us
    ppermute x3, starting transfers between devices, on_device(): got = lax.ppermute(term[middle:], 'section', pairs)  5.76 us
  transfers between devices with their start and end apart: 34, of which 10 were waited for; matrix products, arithmetic and copies ran while one was open for 6% of the time, Pallas kernels for 0%

profile of v1, /device:TPU:6, one launch (start us, length us, event | category | flops | bytes accessed | tf_op | source)
XLA Modules:
  0.0 189.9 jit_solution(12586657422717939339)
XLA Ops:
  1.9 2.1 %collective-permute-start = (bf16[32,512]{1,0:T(8,128)(2,1)S(1)}, bf16[32,512]{1,0:T(8,128)(2,1)S(1)}, u32[]{:S(2)}, u32[]{:S(2)}) collective-permute-start(bf16[32,512]{1,0:T(8,128)(2,1)S(1)} %get-tuple-element.74), channel_id=1, source_target_pairs={{0,1},{1,2},{2,3},{3,4},{4,5},{5,6},{6,7},{7,8},{8,9},{9,10},{10,1... | collective-permute-start | bytes 98312 | tf_op jit(solution)/shard_map/ppermute | solution.py:120
  4.0 3.6 %collective-permute-start.1 = (bf16[32,512]{1,0:T(8,128)(2,1)S(1)}, bf16[32,512]{1,0:T(8,128)(2,1)S(1)}, u32[]{:S(2)}, u32[]{:S(2)}) collective-permute-start(bf16[32,512]{1,0:T(8,128)(2,1)S(1)} %get-tuple-element.73), channel_id=1, source_target_pairs={{0,63},{1,0},{2,1},{3,2},{4,3},{5,4},{6,5},{7,6},{8,7},{9,8},{10,9... | collective-permute-start | bytes 98312 | tf_op jit(solution)/shard_map/ppermute | solution.py:121
  49.5 47.7 %collective-permute-done.22 = bf16[32,512]{1,0:T(8,128)(2,1)S(1)} collective-permute-done((bf16[32,512]{1,0:T(8,128)(2,1)S(1)}, bf16[32,512]{1,0:T(8,128)(2,1)S(1)}, u32[]{:S(2)}, u32[]{:S(2)}) %collective-permute-start.22) | collective-permute-done | bytes 32800 | tf_op jit(solution)/shard_map/ppermute | solution.py:156
  97.2 2.0 %collective-permute-done.21 = bf16[32,512]{1,0:T(8,128)(2,1)S(1)} collective-permute-done((bf16[32,512]{1,0:T(8,128)(2,1)S(1)}, bf16[32,512]{1,0:T(8,128)(2,1)S(1)}, u32[]{:S(2)}, u32[]{:S(2)}) %collective-permute-start.21) | collective-permute-done | bytes 32800 | tf_op jit(solution)/shard_map/ppermute | solution.py:156
  99.2 3.4 %collective-permute-done.20 = bf16[192,512]{1,0:T(8,128)(2,1)S(1)} collective-permute-done((bf16[192,512]{1,0:T(8,128)(2,1)S(1)}, bf16[192,512]{1,0:T(8,128)(2,1)S(1)}, u32[]{:S(2)}, u32[]{:S(2)}) %collective-permute-start.20) | collective-permute-done | bytes 196640 | tf_op jit(solution)/shard_map/ppermute | solution.py:156
  107.4 2.5 %convolution_convert_fusion = bf16[384,512]{1,0:T(8,128)(2,1)} fusion(bf16[384,512]{1,0:T(8,128)(2,1)S(1)} %fusion.8, bf16[1,512,512]{2,1,0:T(8,128)(2,1)} %param.15, s32[384]{0:T(512)S(1)} %copy-done.28), kind=kOutput, calls=%fused_computation.18 | convolution fusion | flops 352862208 | bytes 1312256 | tf_op jit(solution)/shard_map/dot_general | solution.py:84
  110.9 1.9 %collective-permute-start.25 = (bf16[192,512]{1,0:T(8,128)(2,1)S(1)}, bf16[192,512]{1,0:T(8,128)(2,1)S(1)}, u32[]{:S(2)}, u32[]{:S(2)}) collective-permute-start(bf16[192,512]{1,0:T(8,128)(2,1)S(1)} %slice.383), channel_id=1, source_target_pairs={{0,64},{64,0},{128,192},{192,128},{256,320},{320,256},{384,448},{4... | collective-permute-start | bytes 589832 | tf_op jit(solution)/shard_map/ppermute | solution.py:221
  114.2 5.8 %collective-permute-done.25 = bf16[192,512]{1,0:T(8,128)(2,1)S(1)} collective-permute-done((bf16[192,512]{1,0:T(8,128)(2,1)S(1)}, bf16[192,512]{1,0:T(8,128)(2,1)S(1)}, u32[]{:S(2)}, u32[]{:S(2)}) %collective-permute-start.25) | collective-permute-done | bytes 196640 | tf_op jit(solution)/shard_map/ppermute | solution.py:221
  120.1 1.9 %collective-permute-start.26 = (bf16[96,512]{1,0:T(8,128)(2,1)S(1)}, bf16[96,512]{1,0:T(8,128)(2,1)S(1)}, u32[]{:S(2)}, u32[]{:S(2)}) collective-permute-start(bf16[96,512]{1,0:T(8,128)(2,1)S(1)} %slice.385), channel_id=1, source_target_pairs={{0,192},{64,128},{128,64},{192,0},{256,448},{320,384},{384,320},{4... | collective-permute-start | bytes 294920 | tf_op jit(solution)/shard_map/ppermute | solution.py:221
  124.0 2.4 %collective-permute-start.23 = (bf16[32,512]{1,0:T(8,128)(2,1)}, bf16[32,512]{1,0:T(8,128)(2,1)S(1)}, u32[]{:S(2)}, u32[]{:S(2)}) collective-permute-start(bf16[32,512]{1,0:T(8,128)(2,1)} %get-tuple-element.45), channel_id=1, source_target_pairs={{0,1},{1,2},{2,3},{3,4},{4,5},{5,6},{6,7},{7,8},{8,9},{9,10},{10,1... | collective-permute-start | bytes 98312 | tf_op jit(solution)/shard_map/ppermute | solution.py:208
  126.4 2.1 %concatenate.96 = bf16[520,512]{1,0:T(8,128)(2,1)} concatenate(bf16[256,512]{1,0:T(8,128)(2,1)S(1)} %convolution_convert_fusion.4, bf16[256,512]{1,0:T(8,128)(2,1)S(1)} %convolution_convert_fusion.3, bf16[1,512]{1,0:T(2,128)(2,1)S(1)} %convert_element_type.601, bf16[1,512]{1,0:T(2,128)(2,1)S(1)} %subtract_convert_fusion.5, bf16[6,512]{1,0:T(8,128)(2,1)S(1)} %broadcast.139), dimensions={0} | concatenate | bytes 1064960 | tf_op jit(solution)/shard_map/concatenate | solution.py:195
  128.5 4.9 %collective-permute-start.28 = (bf16[520,512]{1,0:T(8,128)(2,1)}, bf16[520,512]{1,0:T(8,128)(2,1)S(1)}, u32[]{:S(2)}, u32[]{:S(2)}) collective-permute-start(bf16[520,512]{1,0:T(8,128)(2,1)} %concatenate.96), channel_id=1, source_target_pairs={{0,1},{1,0},{2,3},{3,2},{4,5},{5,4},{6,7},{7,6},{8,9},{9,8},{10,11... | collective-permute-start | bytes 1597448 | tf_op jit(solution)/shard_map/ppermute | solution.py:195
  133.5 1.9 %collective-permute-start.27 = (bf16[48,512]{1,0:T(8,128)(2,1)S(1)}, bf16[48,512]{1,0:T(8,128)(2,1)S(1)}, u32[]{:S(2)}, u32[]{:S(2)}) collective-permute-start(bf16[48,512]{1,0:T(8,128)(2,1)S(1)} %slice.387), channel_id=1, source_target_pairs={{0,448},{64,384},{128,320},{192,256},{256,192},{320,128},{384,64},... | collective-permute-start | bytes 147464 | tf_op jit(solution)/shard_map/ppermute | solution.py:221
  136.4 5.3 %collective-permute-done.27 = bf16[48,512]{1,0:T(8,128)(2,1)S(1)} collective-permute-done((bf16[48,512]{1,0:T(8,128)(2,1)S(1)}, bf16[48,512]{1,0:T(8,128)(2,1)S(1)}, u32[]{:S(2)}, u32[]{:S(2)}) %collective-permute-start.27) | collective-permute-done | bytes 49184 | tf_op jit(solution)/shard_map/ppermute | solution.py:221
  142.6 2.0 %concatenate.98 = bf16[264,512]{1,0:T(8,128)(2,1)} concatenate(bf16[128,512]{1,0:T(8,128)(2,1)S(1)} %get-tuple-element.38, bf16[128,512]{1,0:T(8,128)(2,1)S(1)} %get-tuple-element.37, bf16[1,512]{1,0:T(2,128)(2,1)S(1)} %convert_element_type.607, bf16[1,512]{1,0:T(2,128)(2,1)S(1)} %get-tuple-element.27, bf16[6,512]{1,0:T(8,128)(2,1)S(1)} %broadcast.139), dimensions={0} | concatenate | bytes 540672 | tf_op jit(solution)/shard_map/concatenate | solution.py:195
  146.5 6.6 %collective-permute-done.29 = bf16[264,512]{1,0:T(8,128)(2,1)S(1)} collective-permute-done((bf16[264,512]{1,0:T(8,128)(2,1)}, bf16[264,512]{1,0:T(8,128)(2,1)S(1)}, u32[]{:S(2)}, u32[]{:S(2)}) %collective-permute-start.29) | collective-permute-done | bytes 270368 | tf_op jit(solution)/shard_map/ppermute | solution.py:195
  153.8 4.3 %collective-permute-start.30 = (bf16[136,512]{1,0:T(8,128)(2,1)S(1)}, bf16[136,512]{1,0:T(8,128)(2,1)S(1)}, u32[]{:S(2)}, u32[]{:S(2)}) collective-permute-start(bf16[136,512]{1,0:T(8,128)(2,1)S(1)} %concatenate.100), channel_id=1, source_target_pairs={{0,8},{1,3},{2,10},{3,1},{4,12},{5,7},{6,14},{7,5},{8,0},{9,11},{1... | collective-permute-start | bytes 417800 | tf_op jit(solution)/shard_map/ppermute | solution.py:195
  158.9 2.2 %collective-permute-done.30 = bf16[136,512]{1,0:T(8,128)(2,1)S(1)} collective-permute-done((bf16[136,512]{1,0:T(8,128)(2,1)S(1)}, bf16[136,512]{1,0:T(8,128)(2,1)S(1)}, u32[]{:S(2)}, u32[]{:S(2)}) %collective-permute-start.30) | collective-permute-done | bytes 139296 | tf_op jit(solution)/shard_map/ppermute | solution.py:195
  161.2 4.0 %collective-permute-start.31 = (bf16[72,512]{1,0:T(8,128)(2,1)S(1)}, bf16[72,512]{1,0:T(8,128)(2,1)S(1)}, u32[]{:S(2)}, u32[]{:S(2)}) collective-permute-start(bf16[72,512]{1,0:T(8,128)(2,1)S(1)} %concatenate.102), channel_id=1, source_target_pairs={{0,6},{1,25},{2,4},{3,27},{4,2},{5,29},{6,0},{7,31},{8,14},{9,17},... | collective-permute-start | bytes 221192 | tf_op jit(solution)/shard_map/ppermute | solution.py:195
  165.3 3.4 %collective-permute-done.31 = bf16[72,512]{1,0:T(8,128)(2,1)S(1)} collective-permute-done((bf16[72,512]{1,0:T(8,128)(2,1)S(1)}, bf16[72,512]{1,0:T(8,128)(2,1)S(1)}, u32[]{:S(2)}, u32[]{:S(2)}) %collective-permute-start.31) | collective-permute-done | bytes 73760 | tf_op jit(solution)/shard_map/ppermute | solution.py:195
  168.8 10.7 %collective-permute-start.32 = (bf16[40,512]{1,0:T(8,128)(2,1)S(1)}, bf16[40,512]{1,0:T(8,128)(2,1)S(1)}, u32[]{:S(2)}, u32[]{:S(2)}) collective-permute-start(bf16[40,512]{1,0:T(8,128)(2,1)S(1)} %concatenate.104), channel_id=1, source_target_pairs={{0,24},{1,7},{2,26},{3,5},{4,28},{5,3},{6,30},{7,1},{8,16},{9,15},... | collective-permute-start | bytes 122888 | tf_op jit(solution)/shard_map/ppermute | solution.py:195
  179.6 1.9 %collective-permute-done.32 = bf16[40,512]{1,0:T(8,128)(2,1)S(1)} collective-permute-done((bf16[40,512]{1,0:T(8,128)(2,1)S(1)}, bf16[40,512]{1,0:T(8,128)(2,1)S(1)}, u32[]{:S(2)}, u32[]{:S(2)}) %collective-permute-start.32) | collective-permute-done | bytes 40992 | tf_op jit(solution)/shard_map/ppermute | solution.py:195
  181.6 3.5 %collective-permute-start.33 = (bf16[24,512]{1,0:T(8,128)(2,1)S(1)}, bf16[24,512]{1,0:T(8,128)(2,1)S(1)}, u32[]{:S(2)}, u32[]{:S(2)}) collective-permute-start(bf16[24,512]{1,0:T(8,128)(2,1)S(1)} %concatenate.106), channel_id=1, source_target_pairs={{0,56},{1,57},{2,58},{3,59},{4,60},{5,61},{6,62},{7,63},{8,48},{9,... | collective-permute-start | bytes 73736 | tf_op jit(solution)/shard_map/ppermute | solution.py:195
  185.1 3.5 %collective-permute-done.33 = bf16[24,512]{1,0:T(8,128)(2,1)S(1)} collective-permute-done((bf16[24,512]{1,0:T(8,128)(2,1)S(1)}, bf16[24,512]{1,0:T(8,128)(2,1)S(1)}, u32[]{:S(2)}, u32[]{:S(2)}) %collective-permute-start.33) | collective-permute-done | bytes 24608 | tf_op jit(solution)/shard_map/ppermute | solution.py:195
  (243 shorter events, 57.5 us)
Async XLA Ops:
  1.9 11.4 %collective-permute-start = (bf16[32,512]{1,0:T(8,128)(2,1)S(1)}, bf16[32,512]{1,0:T(8,128)(2,1)S(1)}, u32[]{:S(2)}, u32[]{:S(2)}) collective-permute-start(bf16[32,512]{1,0:T(8,128)(2,1)S(1)} %get-tuple-element.74), channel_id=1, source_target_pairs={{0,1},{1,2},{2,3},{3,4},{4,5},{5,6},{6,7},{7,8},{8,9},{9,10},{10,1... | collective-permute-start | bytes 98312 | tf_op jit(solution)/shard_map/ppermute | solution.py:120
  4.0 9.4 %collective-permute-start.1 = (bf16[32,512]{1,0:T(8,128)(2,1)S(1)}, bf16[32,512]{1,0:T(8,128)(2,1)S(1)}, u32[]{:S(2)}, u32[]{:S(2)}) collective-permute-start(bf16[32,512]{1,0:T(8,128)(2,1)S(1)} %get-tuple-element.73), channel_id=1, source_target_pairs={{0,63},{1,0},{2,1},{3,2},{4,3},{5,4},{6,5},{7,6},{8,7},{9,8},{10,9... | collective-permute-start | bytes 98312 | tf_op jit(solution)/shard_map/ppermute | solution.py:121
  19.0 2.1 %collective-permute-start.3 = (bf16[32,512]{1,0:T(8,128)(2,1)S(1)}, bf16[32,512]{1,0:T(8,128)(2,1)S(1)}, u32[]{:S(2)}, u32[]{:S(2)}) collective-permute-start(bf16[32,512]{1,0:T(8,128)(2,1)S(1)} %get-tuple-element.60), channel_id=1, source_target_pairs={{448,385},{449,386},{450,387},{451,388},{452,389},{453,390},{454,3... | collective-permute-start | bytes 98312 | tf_op jit(solution)/shard_map/ppermute | solution.py:156
  19.7 1.4 collective-permute-start.4
  23.0 2.1 %collective-permute-start.6 = (bf16[32,512]{1,0:T(8,128)(2,1)S(1)}, bf16[32,512]{1,0:T(8,128)(2,1)S(1)}, u32[]{:S(2)}, u32[]{:S(2)}) collective-permute-start(bf16[32,512]{1,0:T(8,128)(2,1)S(1)} %get-tuple-element.58), channel_id=1, source_target_pairs={{384,321},{385,322},{386,323},{387,324},{388,325},{389,326},{390,3... | collective-permute-start | bytes 98312 | tf_op jit(solution)/shard_map/ppermute | solution.py:156
  26.8 2.1 %collective-permute-start.9 = (bf16[32,512]{1,0:T(8,128)(2,1)S(1)}, bf16[32,512]{1,0:T(8,128)(2,1)S(1)}, u32[]{:S(2)}, u32[]{:S(2)}) collective-permute-start(bf16[32,512]{1,0:T(8,128)(2,1)S(1)} %get-tuple-element.56), channel_id=1, source_target_pairs={{320,257},{321,258},{322,259},{323,260},{324,261},{325,262},{326,2... | collective-permute-start | bytes 98312 | tf_op jit(solution)/shard_map/ppermute | solution.py:156
  30.5 2.1 %collective-permute-start.12 = (bf16[32,512]{1,0:T(8,128)(2,1)S(1)}, bf16[32,512]{1,0:T(8,128)(2,1)S(1)}, u32[]{:S(2)}, u32[]{:S(2)}) collective-permute-start(bf16[32,512]{1,0:T(8,128)(2,1)S(1)} %get-tuple-element.54), channel_id=1, source_target_pairs={{256,193},{257,194},{258,195},{259,196},{260,197},{261,198},{262,1... | collective-permute-start | bytes 98312 | tf_op jit(solution)/shard_map/ppermute | solution.py:156
  34.2 2.1 %collective-permute-start.15 = (bf16[32,512]{1,0:T(8,128)(2,1)S(1)}, bf16[32,512]{1,0:T(8,128)(2,1)S(1)}, u32[]{:S(2)}, u32[]{:S(2)}) collective-permute-start(bf16[32,512]{1,0:T(8,128)(2,1)S(1)} %get-tuple-element.52), channel_id=1, source_target_pairs={{192,129},{193,130},{194,131},{195,132},{196,133},{197,134},{198,1... | collective-permute-start | bytes 98312 | tf_op jit(solution)/shard_map/ppermute | solution.py:156
  39.2 2.3 %collective-permute-start.18 = (bf16[32,512]{1,0:T(8,128)(2,1)S(1)}, bf16[32,512]{1,0:T(8,128)(2,1)S(1)}, u32[]{:S(2)}, u32[]{:S(2)}) collective-permute-start(bf16[32,512]{1,0:T(8,128)(2,1)S(1)} %get-tuple-element.50), channel_id=1, source_target_pairs={{128,65},{129,66},{130,67},{131,68},{132,69},{133,70},{134,71},{13... | collective-permute-start | bytes 98312 | tf_op jit(solution)/shard_map/ppermute | solution.py:156
  40.0 2.3 %collective-permute-start.17 = (bf16[192,512]{1,0:T(8,128)(2,1)S(1)}, bf16[192,512]{1,0:T(8,128)(2,1)S(1)}, u32[]{:S(2)}, u32[]{:S(2)}) collective-permute-start(bf16[192,512]{1,0:T(8,128)(2,1)S(1)} %fusion.82), channel_id=1, source_target_pairs={{128,64},{129,65},{130,66},{131,67},{132,68},{133,69},{134,70},{13... | collective-permute-start | bytes 589832 | tf_op jit(solution)/shard_map/ppermute | solution.py:156
  45.1 52.1 %collective-permute-start.22 = (bf16[32,512]{1,0:T(8,128)(2,1)S(1)}, bf16[32,512]{1,0:T(8,128)(2,1)S(1)}, u32[]{:S(2)}, u32[]{:S(2)}) collective-permute-start(bf16[32,512]{1,0:T(8,128)(2,1)S(1)} %get-tuple-element.48), channel_id=1, source_target_pairs={{64,63},{65,0},{66,1},{67,2},{68,3},{69,4},{70,5},{71,6},{72,7},{7... | collective-permute-start | bytes 98312 | tf_op jit(solution)/shard_map/ppermute | solution.py:156
  46.4 52.8 %collective-permute-start.21 = (bf16[32,512]{1,0:T(8,128)(2,1)S(1)}, bf16[32,512]{1,0:T(8,128)(2,1)S(1)}, u32[]{:S(2)}, u32[]{:S(2)}) collective-permute-start(bf16[32,512]{1,0:T(8,128)(2,1)S(1)} %get-tuple-element.47), channel_id=1, source_target_pairs={{64,1},{65,2},{66,3},{67,4},{68,5},{69,6},{70,7},{71,8},{72,9},{73... | collective-permute-start | bytes 98312 | tf_op jit(solution)/shard_map/ppermute | solution.py:156
  47.8 54.7 %collective-permute-start.20 = (bf16[192,512]{1,0:T(8,128)(2,1)S(1)}, bf16[192,512]{1,0:T(8,128)(2,1)S(1)}, u32[]{:S(2)}, u32[]{:S(2)}) collective-permute-start(bf16[192,512]{1,0:T(8,128)(2,1)S(1)} %fusion.83), channel_id=1, source_target_pairs={{64,0},{65,1},{66,2},{67,3},{68,4},{69,5},{70,6},{71,7},{72,8},{73... | collective-permute-start | bytes 589832 | tf_op jit(solution)/shard_map/ppermute | solution.py:156
  110.9 9.2 %collective-permute-start.25 = (bf16[192,512]{1,0:T(8,128)(2,1)S(1)}, bf16[192,512]{1,0:T(8,128)(2,1)S(1)}, u32[]{:S(2)}, u32[]{:S(2)}) collective-permute-start(bf16[192,512]{1,0:T(8,128)(2,1)S(1)} %slice.383), channel_id=1, source_target_pairs={{0,64},{64,0},{128,192},{192,128},{256,320},{320,256},{384,448},{4... | collective-permute-start | bytes 589832 | tf_op jit(solution)/shard_map/ppermute | solution.py:221
  120.1 13.3 %collective-permute-start.26 = (bf16[96,512]{1,0:T(8,128)(2,1)S(1)}, bf16[96,512]{1,0:T(8,128)(2,1)S(1)}, u32[]{:S(2)}, u32[]{:S(2)}) collective-permute-start(bf16[96,512]{1,0:T(8,128)(2,1)S(1)} %slice.385), channel_id=1, source_target_pairs={{0,192},{64,128},{128,64},{192,0},{256,448},{320,384},{384,320},{4... | collective-permute-start | bytes 294920 | tf_op jit(solution)/shard_map/ppermute | solution.py:221
  122.1 13.4 %collective-permute-start.24 = (bf16[32,512]{1,0:T(8,128)(2,1)}, bf16[32,512]{1,0:T(8,128)(2,1)S(1)}, u32[]{:S(2)}, u32[]{:S(2)}) collective-permute-start(bf16[32,512]{1,0:T(8,128)(2,1)} %get-tuple-element.46), channel_id=1, source_target_pairs={{0,63},{1,0},{2,1},{3,2},{4,3},{5,4},{6,5},{7,6},{8,7},{9,8},{10,9... | collective-permute-start | bytes 98312 | tf_op jit(solution)/shard_map/ppermute | solution.py:209
  124.0 11.5 %collective-permute-start.23 = (bf16[32,512]{1,0:T(8,128)(2,1)}, bf16[32,512]{1,0:T(8,128)(2,1)S(1)}, u32[]{:S(2)}, u32[]{:S(2)}) collective-permute-start(bf16[32,512]{1,0:T(8,128)(2,1)} %get-tuple-element.45), channel_id=1, source_target_pairs={{0,1},{1,2},{2,3},{3,4},{4,5},{5,6},{6,7},{7,8},{8,9},{9,10},{10,1... | collective-permute-start | bytes 98312 | tf_op jit(solution)/shard_map/ppermute | solution.py:208
  128.5 13.7 %collective-permute-start.28 = (bf16[520,512]{1,0:T(8,128)(2,1)}, bf16[520,512]{1,0:T(8,128)(2,1)S(1)}, u32[]{:S(2)}, u32[]{:S(2)}) collective-permute-start(bf16[520,512]{1,0:T(8,128)(2,1)} %concatenate.96), channel_id=1, source_target_pairs={{0,1},{1,0},{2,3},{3,2},{4,5},{5,4},{6,7},{7,6},{8,9},{9,8},{10,11... | collective-permute-start | bytes 1597448 | tf_op jit(solution)/shard_map/ppermute | solution.py:195
  133.5 8.1 %collective-permute-start.27 = (bf16[48,512]{1,0:T(8,128)(2,1)S(1)}, bf16[48,512]{1,0:T(8,128)(2,1)S(1)}, u32[]{:S(2)}, u32[]{:S(2)}) collective-permute-start(bf16[48,512]{1,0:T(8,128)(2,1)S(1)} %slice.387), channel_id=1, source_target_pairs={{0,448},{64,384},{128,320},{192,256},{256,192},{320,128},{384,64},... | collective-permute-start | bytes 147464 | tf_op jit(solution)/shard_map/ppermute | solution.py:221
  144.5 8.6 %collective-permute-start.29 = (bf16[264,512]{1,0:T(8,128)(2,1)}, bf16[264,512]{1,0:T(8,128)(2,1)S(1)}, u32[]{:S(2)}, u32[]{:S(2)}) collective-permute-start(bf16[264,512]{1,0:T(8,128)(2,1)} %concatenate.98), channel_id=1, source_target_pairs={{0,2},{1,9},{2,0},{3,11},{4,6},{5,13},{6,4},{7,15},{8,10},{9,1},{1... | collective-permute-start | bytes 811016 | tf_op jit(solution)/shard_map/ppermute | solution.py:195
  153.8 7.3 %collective-permute-start.30 = (bf16[136,512]{1,0:T(8,128)(2,1)S(1)}, bf16[136,512]{1,0:T(8,128)(2,1)S(1)}, u32[]{:S(2)}, u32[]{:S(2)}) collective-permute-start(bf16[136,512]{1,0:T(8,128)(2,1)S(1)} %concatenate.100), channel_id=1, source_target_pairs={{0,8},{1,3},{2,10},{3,1},{4,12},{5,7},{6,14},{7,5},{8,0},{9,11},{1... | collective-permute-start | bytes 417800 | tf_op jit(solution)/shard_map/ppermute | solution.py:195
  161.2 7.5 %collective-permute-start.31 = (bf16[72,512]{1,0:T(8,128)(2,1)S(1)}, bf16[72,512]{1,0:T(8,128)(2,1)S(1)}, u32[]{:S(2)}, u32[]{:S(2)}) collective-permute-start(bf16[72,512]{1,0:T(8,128)(2,1)S(1)} %concatenate.102), channel_id=1, source_target_pairs={{0,6},{1,25},{2,4},{3,27},{4,2},{5,29},{6,0},{7,31},{8,14},{9,17},... | collective-permute-start | bytes 221192 | tf_op jit(solution)/shard_map/ppermute | solution.py:195
  168.8 12.7 %collective-permute-start.32 = (bf16[40,512]{1,0:T(8,128)(2,1)S(1)}, bf16[40,512]{1,0:T(8,128)(2,1)S(1)}, u32[]{:S(2)}, u32[]{:S(2)}) collective-permute-start(bf16[40,512]{1,0:T(8,128)(2,1)S(1)} %concatenate.104), channel_id=1, source_target_pairs={{0,24},{1,7},{2,26},{3,5},{4,28},{5,3},{6,30},{7,1},{8,16},{9,15},... | collective-permute-start | bytes 122888 | tf_op jit(solution)/shard_map/ppermute | solution.py:195
  181.6 7.1 %collective-permute-start.33 = (bf16[24,512]{1,0:T(8,128)(2,1)S(1)}, bf16[24,512]{1,0:T(8,128)(2,1)S(1)}, u32[]{:S(2)}, u32[]{:S(2)}) collective-permute-start(bf16[24,512]{1,0:T(8,128)(2,1)S(1)} %concatenate.106), channel_id=1, source_target_pairs={{0,56},{1,57},{2,58},{3,59},{4,60},{5,61},{6,62},{7,63},{8,48},{9,... | collective-permute-start | bytes 73736 | tf_op jit(solution)/shard_map/ppermute | solution.py:195
  (41 other events, 183.8 us)

commit v2 on v1

v2 whole, which is shorter than its diff:
```python
import numpy as np
import jax
import jax.numpy as jnp
from jax import lax
from jax.sharding import PartitionSpec as P

EDGE_BLOCK = 128
NORM_EPSILON = 1e-05

ALONG_X = [[z * 8 + x * 2 + c for x in range(4)] for z in range(8) for c in range(2)]
ALONG_Z = [[z * 8 + x * 2 + c for z in range(8)] for x in range(4) for c in range(2)]


def section_order(sections):
    table = np.zeros((sections, sections), np.int32)
    for s in range(sections):
        for j in range(sections):
            table[s, j] = s ^ sum(((j >> (2 - k)) & 1) << k for k in range(3))
    return table


def after(mark, *values):
    return lax.optimization_barrier((mark, *values))[1:]


def onehot(index, count):
    return (index[:, None] == jnp.arange(count, dtype=jnp.int32)[None, :]).astype(jnp.bfloat16)


def onehot_t(index, count):
    return (jnp.arange(count, dtype=jnp.int32)[:, None] == index[None, :]).astype(jnp.bfloat16)


def dot(a, b):
    return jnp.dot(a, b, preferred_element_type=jnp.float32)


def dot_t(a, b):
    return lax.dot_general(a, b, (((1,), (1,)), ((), ())), preferred_element_type=jnp.float32)


def spread(chunks, size):
    return (chunks[:, None] * size + jnp.arange(size, dtype=jnp.int32)[None, :]).reshape(-1)


def on_device(
    node_states,
    edge_features,
    out_cotangent,
    edge_weight,
    send_weight,
    layer_norm_gain,
    edge_sender,
    edge_receiver,
    halo_rows,
    block_counts,
):
    bf16, f32 = jnp.bfloat16, jnp.float32
    h = node_states[0, 0]
    feats = edge_features[0]
    w_edge, w_send, gain = edge_weight[0], send_weight[0], layer_norm_gain[0]
    nodes, width = h.shape
    edges = feats.shape[0]
    rim = halo_rows.shape[0] // 2
    rows = nodes + 2 * rim
    sections, doms = lax.axis_size("section"), lax.axis_size("dom")
    section, dom = lax.axis_index("section"), lax.axis_index("dom")

    near = [p ^ 1 for p in range(doms)]
    far = [(p + 1) % doms if p % 2 else (p - 1) % doms for p in range(doms)]
    near_pairs, far_pairs = list(enumerate(near)), list(enumerate(far))
    even = dom % 2 == 0
    label = jnp.arange(rows, dtype=jnp.int32)
    label = jnp.where(even & (label >= nodes), nodes + (label - nodes + rim) % (2 * rim), label)

    picks = jnp.concatenate([halo_rows, jnp.arange(nodes, dtype=jnp.int32)])
    chosen = lax.optimization_barrier(dot(onehot(picks, nodes), h).astype(bf16))
    from_far = lax.ppermute(jnp.where(even, chosen[:rim], chosen[rim : 2 * rim]), "dom", far_pairs)
    from_near = lax.ppermute(jnp.where(even, chosen[rim : 2 * rim], chosen[:rim]), "dom", near_pairs)
    h_rim = jnp.concatenate([from_near, from_far], axis=0)
    send_hot = (edge_sender[:, None] == label[None, :]).astype(bf16)
    send_hot_t = (label[:, None] == edge_sender[None, :]).astype(bf16)
    recv_hot = onehot(edge_receiver, nodes)
    recv_hot_t = onehot_t(edge_receiver, nodes)
    live = (jnp.arange(edges, dtype=jnp.int32) // EDGE_BLOCK < block_counts[0]).astype(f32)[:, None]
    own = dot(chosen[2 * rim :], w_send).astype(bf16)
    base = lax.optimization_barrier(dot(feats, w_edge) + dot(send_hot[:, :nodes], own))
    pre = lax.optimization_barrier(base + dot(send_hot[:, nodes:], dot(h_rim, w_send).astype(bf16)))
    sig = jax.nn.sigmoid(pre)
    message = (live * (pre * sig)).astype(bf16)
    slope = live * (sig * (1.0 + pre * (1.0 - sig)))
    slope = lax.optimization_barrier(slope)
    agg = dot(recv_hot_t, message)
    scale = lax.rsqrt(jnp.mean(agg * agg, axis=-1, keepdims=True) + NORM_EPSILON)
    normed = agg * scale

    def backward(up):
        up_wide = up.astype(f32)
        dnorm = up_wide * gain
        dagg = scale * (dnorm - normed * jnp.mean(dnorm * normed, axis=-1, keepdims=True))
        gathered = dot(recv_hot, dagg.astype(bf16))
        dpre = (slope * gathered).astype(bf16)
        return dpre, dot(send_hot_t, dpre).astype(bf16)

    def own_part(up, table):
        return (up.astype(f32) + dot_t(table[:nodes], w_send)).astype(bf16)

    def rim_part(table):
        return dot_t(table[nodes:], w_send).astype(bf16)

    def joined(part, from_near, from_far):
        (from_far,) = after(part, from_far)
        total = lax.optimization_barrier(part.astype(f32) + dot(far_t, from_far))
        (from_near,) = after(total, from_near)
        return (total + dot(near_t, from_near)).astype(bf16)

    def hop(value, t, target):
        top = sections - 1 - t
        pairs = [(top * doms + p, (top - 1) * doms + target[p]) for p in range(doms)]
        return lax.ppermute(value, ("section", "dom"), pairs)

    up = out_cotangent[0]
    held = jnp.where(section == sections - 1, up, jnp.zeros_like(up))
    for t in range(sections - 1):
        _, table = backward(up)
        rims = rim_part(table)
        part = own_part(up, table)
        if t == 0:
            (rows_late,) = after(part, halo_rows)
            near_t = onehot_t(jnp.where(even, rows_late[rim:], rows_late[:rim]), nodes)
            far_t = onehot_t(jnp.where(even, rows_late[:rim], rows_late[rim:]), nodes)
        from_far = hop(rims[rim:], t, far)
        from_near = hop(rims[:rim], t, near)
        up = joined(hop(part, t, range(doms)), from_near, from_far)
        if t == sections - 3:
            feats_late, h_late, h_rim_late, dom_late, section_late = after(part, feats, h, h_rim, dom, section)
            place = jnp.arange(doms, dtype=jnp.int32)
            chunk = (place % 8) * 8 + (place // 8 % 4) * 2 + (dom_late + place // 32) % 2
            mixer = onehot(spread(chunk, width // doms), width)
            feats_t = dot_t(mixer, feats_late).astype(bf16)
            h_t = jnp.concatenate([dot_t(mixer, h_late), dot_t(mixer, h_rim_late)], axis=1).astype(bf16)
            s_order = lax.dynamic_index_in_dim(jnp.asarray(section_order(sections)), section_late, 0, keepdims=False)
            s_order = spread(s_order, edges // sections)
            up, mixer, feats_t, h_t, s_order = lax.optimization_barrier((up, mixer, feats_t, h_t, s_order))
        if t < sections - 2:
            held = held + up
            held, up = lax.optimization_barrier((held, up))

    up = held + up
    dpre, table = backward(up)
    gain_part = jnp.sum(up.astype(f32) * normed, axis=0)

    def section_send(term, k):
        pairs = [(s, s ^ (1 << k)) for s in range(sections)]
        return lax.ppermute(term[term.shape[0] // 2 :], "section", pairs)

    def section_add(term, got):
        return (term[: term.shape[0] // 2].astype(f32) + got.astype(f32)).astype(bf16)

    half = width // 2
    gain_rows = jnp.broadcast_to(gain_part.astype(bf16)[None], (128, width))

    def gradients(at):
        return jnp.concatenate([dot(feats_t[at], dpre), dot(h_t[at], table), dot_t(mixer[at], gain_rows)], axis=1)

    rims = rim_part(table)
    beside = jnp.pad(rims[:rim], ((0, 0), (0, width + 128)))
    payload = jnp.concatenate([gradients(slice(half, width)).astype(bf16), beside], axis=0)
    got = lax.ppermute(payload, "dom", near_pairs)
    (dpre_late,) = after(payload, dpre)
    term = dot_t(dot(onehot(s_order, edges), dpre_late).astype(bf16), w_edge).astype(bf16)
    section_got = section_send(term, 0)
    from_near = got[half:, :width]
    sums = gradients(slice(0, half)) + got[:half].astype(f32)
    (sums,) = after(term, sums.astype(bf16))

    term, section_got = after(sums, term, section_got)
    sums = lax.all_to_all(sums.reshape(4, half // 4, -1), "dom", 0, 0, axis_index_groups=ALONG_X)
    term = section_add(term, section_got)
    section_got = section_send(term, 1)
    sums = jnp.sum(sums.astype(f32), axis=0).astype(bf16)
    (sums,) = after(term, sums)

    term, section_got, rims, table, up = after(sums, term, section_got, rims, table, up)
    sums = lax.all_to_all(sums.reshape(8, half // 32, -1), "dom", 0, 0, axis_index_groups=ALONG_Z)
    term = section_add(term, section_got)
    section_got = section_send(term, 2)
    from_far = lax.ppermute(rims[rim:], "dom", far_pairs)
    part = own_part(up, table)
    (sums,) = after(term, sums)
    sums = jnp.sum(sums.astype(f32), axis=0)

    node_grads = joined(part, from_near, from_far)
    edge_grad, send_grad, gain_grad = sums[:, :width], sums[:, width : 2 * width], sums[:, 2 * width]
    term = section_add(term, section_got)

    return (
        node_grads[None, None],
        term[None],
        edge_grad[None],
        send_grad[None],
        gain_grad[None],
    )


def solution(mesh):
    return jax.shard_map(
        on_device,
        mesh=mesh,
        in_specs=(
            P("section", None, "dom", None),
            P(None, "dom", None),
            P(None, "dom", None),
            P("section", None, None),
            P("section", None, None),
            P("section", None),
            P("dom"),
            P("dom"),
            P("dom"),
            P("dom"),
        ),
        out_specs=(
            P("section", None, "dom", None),
            P(None, ("dom", "section"), None),
            P("section", "dom", None),
            P("section", "dom", None),
            P("section", "dom"),
        ),
        check_vma=False,
    )
```

time: 191 us -> 154 us (0.81)
  the two profiles are of different devices: /device:TPU:6 before, /device:TPU:1 now
where the time goes in v2:
time: 154 us; the launch traced here: 153 us
  waiting for transfers between devices  61.6 us (40%)
  starting transfers between devices  47.2 us (31%)
  matrix products  24.9 us (16%)
  other arithmetic  10.5 us (7%)
  local copies, waits for them, and re-layouts  6.39 us (4%)
  between operations  2.46 us (2%)
    ppermute x21, waiting for transfers between devices, hop(): return lax.ppermute(value, ('section', 'dom'), pairs)  47.1 us
    ppermute x21, starting transfers between devices, hop(): return lax.ppermute(value, ('section', 'dom'), pairs)  16.6 us
    dot_general x34, matrix products, dot(): return jnp.dot(a, b, preferred_element_type=jnp.float32)  13.8 us
    dot_general x22, matrix products, dot_t(): lax.dot_general(a, b, (((1,), (1,)), ((), ())), preferred_element_type=jn...  11.1 us
    ppermute x1, starting transfers between devices, on_device(): lax.ppermute(jnp.where(even, chosen[rim:2 * rim], chosen[:rim]), 'dom', n...  8.79 us
    all_to_all x1, waiting for transfers between devices, on_device(): lax.all_to_all(sums.reshape(4, half // 4, -1), 'dom', 0, 0, axis_index_gr...  6.61 us
    ppermute x3, starting transfers between devices, section_send(): return lax.ppermute(term[term.shape[0] // 2:], 'section', pairs)  5.89 us
    all_to_all x1, waiting for transfers between devices, on_device(): lax.all_to_all(sums.reshape(8, half // 32, -1), 'dom', 0, 0, axis_index_g...  5.04 us
  transfers between devices with their start and end apart: 30, of which 7 were waited for; matrix products, arithmetic and copies ran while one was open for 14% of the time, Pallas kernels for 0%

profile of v2, /device:TPU:1, one launch (start us, length us, event | category | flops | bytes accessed | tf_op | source)
XLA Modules:
  0.0 153.1 jit_solution(10377597624142852991)
XLA Ops:
  1.5 1.2 convolution_convert_fusion.13
  2.7 8.8 %collective-permute-start = (bf16[32,512]{1,0:T(8,128)(2,1)S(1)}, bf16[32,512]{1,0:T(8,128)(2,1)S(1)}, u32[]{:S(2)}, u32[]{:S(2)}) collective-permute-start(bf16[32,512]{1,0:T(8,128)(2,1)S(1)} %get-tuple-element.108), channel_id=1, source_target_pairs={{0,1},{1,0},{2,3},{3,2},{4,5},{5,4},{6,7},{7,6},{8,9},{9,8},{10,11... | collective-permute-start | bytes 98312 | tf_op jit(solution)/shard_map/ppermute | solution.py:79
  11.5 1.9 %collective-permute-start.1 = (bf16[32,512]{1,0:T(8,128)(2,1)S(1)}, bf16[32,512]{1,0:T(8,128)(2,1)S(1)}, u32[]{:S(2)}, u32[]{:S(2)}) collective-permute-start(bf16[32,512]{1,0:T(8,128)(2,1)S(1)} %get-tuple-element.107), channel_id=1, source_target_pairs={{0,63},{1,2},{2,1},{3,4},{4,3},{5,6},{6,5},{7,8},{8,7},{9,10},{10,... | collective-permute-start | bytes 98312 | tf_op jit(solution)/shard_map/ppermute | solution.py:78
  41.4 1.3 collective-permute-start.18
  44.3 1.7 %fusion.36 = bf16[512,512]{1,0:T(8,128)(2,1)} fusion(s32[512]{0:T(512)} %add.330), kind=kLoop, calls=%fused_computation.92 | loop fusion | flops 524288 | bytes 526336 | tf_op jit(solution)/shard_map/convert_element_type | solution.py:27
  46.0 1.9 %convolution_convert_fusion.2 = bf16[512,384]{1,0:T(8,128)(2,1)} fusion(bf16[384,512]{1,0:T(8,128)(2,1)S(1)} %bitcast.121, s32[512]{0:T(512)} %add.330), kind=kOutput, calls=%fused_computation.22 | convolution fusion | flops 201785344 | bytes 788480 | tf_op jit(solution)/shard_map/dot_general | solution.py:39
  54.5 1.3 collective-permute-start.20
  55.9 1.3 collective-permute-start.21
  57.2 1.3 collective-permute-start.22
  58.5 41.5 %collective-permute-done.21 = bf16[32,512]{1,0:T(8,128)(2,1)S(1)} collective-permute-done((bf16[32,512]{1,0:T(8,128)(2,1)S(1)}, bf16[32,512]{1,0:T(8,128)(2,1)S(1)}, u32[]{:S(2)}, u32[]{:S(2)}) %collective-permute-start.21) | collective-permute-done | bytes 32800 | tf_op jit(solution)/shard_map/ppermute | solution.py:120
  99.9 1.8 %collective-permute-done.20 = bf16[192,512]{1,0:T(8,128)(2,1)S(1)} collective-permute-done((bf16[192,512]{1,0:T(8,128)(2,1)S(1)}, bf16[192,512]{1,0:T(8,128)(2,1)S(1)}, u32[]{:S(2)}, u32[]{:S(2)}) %collective-permute-start.20) | collective-permute-done | bytes 196640 | tf_op jit(solution)/shard_map/ppermute | solution.py:120
  101.9 3.8 %collective-permute-done.22 = bf16[32,512]{1,0:T(8,128)(2,1)S(1)} collective-permute-done((bf16[32,512]{1,0:T(8,128)(2,1)S(1)}, bf16[32,512]{1,0:T(8,128)(2,1)S(1)}, u32[]{:S(2)}, u32[]{:S(2)}) %collective-permute-start.22) | collective-permute-done | bytes 32800 | tf_op jit(solution)/shard_map/ppermute | solution.py:120
  108.5 3.8 %collective-permute-start.23 = (bf16[288,1152]{1,0:T(8,128)(2,1)S(1)}, bf16[288,1152]{1,0:T(8,128)(2,1)}, u32[]{:S(2)}, u32[]{:S(2)}) collective-permute-start(bf16[288,1152]{1,0:T(8,128)(2,1)S(1)} %fusion.37), channel_id=1, source_target_pairs={{0,1},{1,0},{2,3},{3,2},{4,5},{5,4},{6,7},{7,6},{8,9},{9,8},{10,11... | collective-permute-start | bytes 1990664 | tf_op jit(solution)/shard_map/ppermute | solution.py:169
  113.0 2.1 %collective-permute-start.24 = (bf16[192,512]{1,0:T(8,128)(2,1)S(1)}, bf16[192,512]{1,0:T(8,128)(2,1)}, u32[]{:S(2)}, u32[]{:S(2)}) collective-permute-start(bf16[192,512]{1,0:T(8,128)(2,1)S(1)} %slice.264), channel_id=1, source_target_pairs={{0,64},{64,0},{128,192},{192,128},{256,320},{320,256},{384,448},{4... | collective-permute-start | bytes 589832 | tf_op jit(solution)/shard_map/ppermute | solution.py:155
  115.1 1.2 fusion.109
  116.9 2.1 %fusion.9 = bf16[256,1152]{1,0:T(8,128)(2,1)} fusion(f32[256,128]{1,0:T(8,128)S(1)} %fusion.109, f32[256,512]{1,0:T(8,128)S(1)} %fusion.224, f32[256,512]{1,0:T(8,128)S(1)} %fusion.143, bf16[288,1152]{1,0:T(8,128)(2,1)} %collective-permute-done.23), kind=kLoop, calls=%fused_computation.51 | loop fusion | flops 1474560 | bytes 2359296 | tf_op jit(solution)/shard_map/convert_element_type | solution.py:175
  118.9 3.5 %all-to-all-start = ((bf16[4,64,1152]{2,1,0:T(8,128)(2,1)}), bf16[4,64,1152]{2,1,0:T(8,128)(2,1)S(1)}, u32[]{:S(2)}, u32[]{:S(2)}) async-start(bf16[4,64,1152]{2,1,0:T(8,128)(2,1)} %bitcast.10), calls=%async_computation | async-start | bytes 1179648 | tf_op jit(solution)/shard_map/all_to_all | solution.py:178
  123.4 1.9 %collective-permute-start.25 = (bf16[96,512]{1,0:T(8,128)(2,1)S(1)}, bf16[96,512]{1,0:T(8,128)(2,1)S(1)}, u32[]{:S(2)}, u32[]{:S(2)}) collective-permute-start(bf16[96,512]{1,0:T(8,128)(2,1)S(1)} %slice.265), channel_id=1, source_target_pairs={{0,128},{64,192},{128,0},{192,64},{256,384},{320,448},{384,256},{4... | collective-permute-start | bytes 294920 | tf_op jit(solution)/shard_map/ppermute | solution.py:155
  126.1 6.6 %all-to-all-done = bf16[4,64,1152]{2,1,0:T(8,128)(2,1)S(1)} async-done(((bf16[4,64,1152]{2,1,0:T(8,128)(2,1)}), bf16[4,64,1152]{2,1,0:T(8,128)(2,1)S(1)}, u32[]{:S(2)}, u32[]{:S(2)}) %all-to-all-start) | async-done | bytes 589856 | tf_op jit(solution)/shard_map/all_to_all | solution.py:178
  133.5 3.2 %collective-permute-start.26 = (bf16[32,512]{1,0:T(8,128)(2,1)S(1)}, bf16[32,512]{1,0:T(8,128)(2,1)S(1)}, u32[]{:S(2)}, u32[]{:S(2)}) collective-permute-start(bf16[32,512]{1,0:T(8,128)(2,1)S(1)} %slice.220), channel_id=1, source_target_pairs={{0,63},{1,2},{2,1},{3,4},{4,3},{5,6},{6,5},{7,8},{8,7},{9,10},{10,... | collective-permute-start | bytes 98312 | tf_op jit(solution)/shard_map/ppermute | solution.py:188
  136.8 1.9 %collective-permute-start.27 = (bf16[48,512]{1,0:T(8,128)(2,1)S(1)}, bf16[48,512]{1,0:T(8,128)(2,1)S(1)}, u32[]{:S(2)}, u32[]{:S(2)}) collective-permute-start(bf16[48,512]{1,0:T(8,128)(2,1)S(1)} %slice.268), channel_id=1, source_target_pairs={{0,256},{64,320},{128,384},{192,448},{256,0},{320,64},{384,128},{4... | collective-permute-start | bytes 147464 | tf_op jit(solution)/shard_map/ppermute | solution.py:155
  138.7 3.4 %all-to-all-start.1 = ((bf16[8,8,1152]{2,1,0:T(8,128)(2,1)}), bf16[8,8,1152]{2,1,0:T(8,128)(2,1)S(1)}, u32[]{:S(2)}, u32[]{:S(2)}) async-start(bf16[8,8,1152]{2,1,0:T(8,128)(2,1)} %bitcast.13), calls=%async_computation.1 | async-start | bytes 294912 | tf_op jit(solution)/shard_map/all_to_all | solution.py:185
  143.5 2.6 %collective-permute-done.27 = bf16[48,512]{1,0:T(8,128)(2,1)S(1)} collective-permute-done((bf16[48,512]{1,0:T(8,128)(2,1)S(1)}, bf16[48,512]{1,0:T(8,128)(2,1)S(1)}, u32[]{:S(2)}, u32[]{:S(2)}) %collective-permute-start.27) | collective-permute-done | bytes 49184 | tf_op jit(solution)/shard_map/ppermute | solution.py:155
  146.8 5.0 %all-to-all-done.1 = bf16[8,8,1152]{2,1,0:T(8,128)(2,1)S(1)} async-done(((bf16[8,8,1152]{2,1,0:T(8,128)(2,1)}), bf16[8,8,1152]{2,1,0:T(8,128)(2,1)S(1)}, u32[]{:S(2)}, u32[]{:S(2)}) %all-to-all-start.1) | async-done | bytes 147488 | tf_op jit(solution)/shard_map/all_to_all | solution.py:185
  (201 shorter events, 45.5 us)
Async XLA Ops:
  2.7 13.8 %collective-permute-start = (bf16[32,512]{1,0:T(8,128)(2,1)S(1)}, bf16[32,512]{1,0:T(8,128)(2,1)S(1)}, u32[]{:S(2)}, u32[]{:S(2)}) collective-permute-start(bf16[32,512]{1,0:T(8,128)(2,1)S(1)} %get-tuple-element.108), channel_id=1, source_target_pairs={{0,1},{1,0},{2,3},{3,2},{4,5},{5,4},{6,7},{7,6},{8,9},{9,8},{10,11... | collective-permute-start | bytes 98312 | tf_op jit(solution)/shard_map/ppermute | solution.py:79
  11.5 5.2 %collective-permute-start.1 = (bf16[32,512]{1,0:T(8,128)(2,1)S(1)}, bf16[32,512]{1,0:T(8,128)(2,1)S(1)}, u32[]{:S(2)}, u32[]{:S(2)}) collective-permute-start(bf16[32,512]{1,0:T(8,128)(2,1)S(1)} %get-tuple-element.107), channel_id=1, source_target_pairs={{0,63},{1,2},{2,1},{3,4},{4,3},{5,6},{6,5},{7,8},{8,7},{9,10},{10,... | collective-permute-start | bytes 98312 | tf_op jit(solution)/shard_map/ppermute | solution.py:78
  20.4 2.1 %collective-permute-start.2 = (bf16[192,512]{1,0:T(8,128)(2,1)S(1)}, bf16[192,512]{1,0:T(8,128)(2,1)S(1)}, u32[]{:S(2)}, u32[]{:S(2)}) collective-permute-start(bf16[192,512]{1,0:T(8,128)(2,1)S(1)} %fusion.18), channel_id=1, source_target_pairs={{448,384},{449,385},{450,386},{451,387},{452,388},{453,389},{454,3... | collective-permute-start | bytes 589832 | tf_op jit(solution)/shard_map/ppermute | solution.py:120
  21.1 1.4 collective-permute-start.3
  24.4 2.0 %collective-permute-start.5 = (bf16[192,512]{1,0:T(8,128)(2,1)S(1)}, bf16[192,512]{1,0:T(8,128)(2,1)S(1)}, u32[]{:S(2)}, u32[]{:S(2)}) collective-permute-start(bf16[192,512]{1,0:T(8,128)(2,1)S(1)} %fusion.19), channel_id=1, source_target_pairs={{384,320},{385,321},{386,322},{387,323},{388,324},{389,325},{390,3... | collective-permute-start | bytes 589832 | tf_op jit(solution)/shard_map/ppermute | solution.py:120
  25.1 1.3 collective-permute-start.6
  28.3 2.0 %collective-permute-start.8 = (bf16[192,512]{1,0:T(8,128)(2,1)S(1)}, bf16[192,512]{1,0:T(8,128)(2,1)S(1)}, u32[]{:S(2)}, u32[]{:S(2)}) collective-permute-start(bf16[192,512]{1,0:T(8,128)(2,1)S(1)} %fusion.20), channel_id=1, source_target_pairs={{320,256},{321,257},{322,258},{323,259},{324,260},{325,261},{326,2... | collective-permute-start | bytes 589832 | tf_op jit(solution)/shard_map/ppermute | solution.py:120
  32.2 2.0 %collective-permute-start.11 = (bf16[192,512]{1,0:T(8,128)(2,1)S(1)}, bf16[192,512]{1,0:T(8,128)(2,1)S(1)}, u32[]{:S(2)}, u32[]{:S(2)}) collective-permute-start(bf16[192,512]{1,0:T(8,128)(2,1)S(1)} %fusion.21), channel_id=1, source_target_pairs={{256,192},{257,193},{258,194},{259,195},{260,196},{261,197},{262,1... | collective-permute-start | bytes 589832 | tf_op jit(solution)/shard_map/ppermute | solution.py:120
  32.9 1.3 collective-permute-start.12
  36.1 2.0 %collective-permute-start.14 = (bf16[192,512]{1,0:T(8,128)(2,1)S(1)}, bf16[192,512]{1,0:T(8,128)(2,1)S(1)}, u32[]{:S(2)}, u32[]{:S(2)}) collective-permute-start(bf16[192,512]{1,0:T(8,128)(2,1)S(1)} %fusion.22), channel_id=1, source_target_pairs={{192,128},{193,129},{194,130},{195,131},{196,132},{197,133},{198,1... | collective-permute-start | bytes 589832 | tf_op jit(solution)/shard_map/ppermute | solution.py:120
  36.8 1.3 collective-permute-start.15
  40.1 11.6 %collective-permute-start.17 = (bf16[192,512]{1,0:T(8,128)(2,1)S(1)}, bf16[192,512]{1,0:T(8,128)(2,1)S(1)}, u32[]{:S(2)}, u32[]{:S(2)}) collective-permute-start(bf16[192,512]{1,0:T(8,128)(2,1)S(1)} %fusion.23), channel_id=1, source_target_pairs={{128,64},{129,65},{130,66},{131,67},{132,68},{133,69},{134,70},{13... | collective-permute-start | bytes 589832 | tf_op jit(solution)/shard_map/ppermute | solution.py:120
  41.4 10.3 %collective-permute-start.18 = (bf16[32,512]{1,0:T(8,128)(2,1)}, bf16[32,512]{1,0:T(8,128)(2,1)}, u32[]{:S(2)}, u32[]{:S(2)}) collective-permute-start(bf16[32,512]{1,0:T(8,128)(2,1)} %get-tuple-element.112), channel_id=1, source_target_pairs={{128,127},{129,66},{130,65},{131,68},{132,67},{133,70},{134,69},{1... | collective-permute-start | bytes 98312 | tf_op jit(solution)/shard_map/ppermute | solution.py:120
  42.7 10.0 %collective-permute-start.19 = (bf16[32,512]{1,0:T(8,128)(2,1)}, bf16[32,512]{1,0:T(8,128)(2,1)S(1)}, u32[]{:S(2)}, u32[]{:S(2)}) collective-permute-start(bf16[32,512]{1,0:T(8,128)(2,1)} %get-tuple-element.111), channel_id=1, source_target_pairs={{128,65},{129,64},{130,67},{131,66},{132,69},{133,68},{134,71},{13... | collective-permute-start | bytes 98312 | tf_op jit(solution)/shard_map/ppermute | solution.py:120
  54.5 47.2 %collective-permute-start.20 = (bf16[192,512]{1,0:T(8,128)(2,1)S(1)}, bf16[192,512]{1,0:T(8,128)(2,1)S(1)}, u32[]{:S(2)}, u32[]{:S(2)}) collective-permute-start(bf16[192,512]{1,0:T(8,128)(2,1)S(1)} %fusion.24), channel_id=1, source_target_pairs={{64,0},{65,1},{66,2},{67,3},{68,4},{69,5},{70,6},{71,7},{72,8},{73... | collective-permute-start | bytes 589832 | tf_op jit(solution)/shard_map/ppermute | solution.py:120
  55.9 44.1 %collective-permute-start.21 = (bf16[32,512]{1,0:T(8,128)(2,1)S(1)}, bf16[32,512]{1,0:T(8,128)(2,1)S(1)}, u32[]{:S(2)}, u32[]{:S(2)}) collective-permute-start(bf16[32,512]{1,0:T(8,128)(2,1)S(1)} %get-tuple-element.110), channel_id=1, source_target_pairs={{64,63},{65,2},{66,1},{67,4},{68,3},{69,6},{70,5},{71,8},{72,7},{7... | collective-permute-start | bytes 98312 | tf_op jit(solution)/shard_map/ppermute | solution.py:120
  57.2 48.5 %collective-permute-start.22 = (bf16[32,512]{1,0:T(8,128)(2,1)S(1)}, bf16[32,512]{1,0:T(8,128)(2,1)S(1)}, u32[]{:S(2)}, u32[]{:S(2)}) collective-permute-start(bf16[32,512]{1,0:T(8,128)(2,1)S(1)} %get-tuple-element.109), channel_id=1, source_target_pairs={{64,1},{65,0},{66,3},{67,2},{68,5},{69,4},{70,7},{71,6},{72,9},{73... | collective-permute-start | bytes 98312 | tf_op jit(solution)/shard_map/ppermute | solution.py:120
  108.5 8.4 %collective-permute-start.23 = (bf16[288,1152]{1,0:T(8,128)(2,1)S(1)}, bf16[288,1152]{1,0:T(8,128)(2,1)}, u32[]{:S(2)}, u32[]{:S(2)}) collective-permute-start(bf16[288,1152]{1,0:T(8,128)(2,1)S(1)} %fusion.37), channel_id=1, source_target_pairs={{0,1},{1,0},{2,3},{3,2},{4,5},{5,4},{6,7},{7,6},{8,9},{9,8},{10,11... | collective-permute-start | bytes 1990664 | tf_op jit(solution)/shard_map/ppermute | solution.py:169
  113.0 9.4 %collective-permute-start.24 = (bf16[192,512]{1,0:T(8,128)(2,1)S(1)}, bf16[192,512]{1,0:T(8,128)(2,1)}, u32[]{:S(2)}, u32[]{:S(2)}) collective-permute-start(bf16[192,512]{1,0:T(8,128)(2,1)S(1)} %slice.264), channel_id=1, source_target_pairs={{0,64},{64,0},{128,192},{192,128},{256,320},{320,256},{384,448},{4... | collective-permute-start | bytes 589832 | tf_op jit(solution)/shard_map/ppermute | solution.py:155
  118.9 13.8 %all-to-all-start = ((bf16[4,64,1152]{2,1,0:T(8,128)(2,1)}), bf16[4,64,1152]{2,1,0:T(8,128)(2,1)S(1)}, u32[]{:S(2)}, u32[]{:S(2)}) async-start(bf16[4,64,1152]{2,1,0:T(8,128)(2,1)} %bitcast.10), calls=%async_computation | async-start | bytes 1179648 | tf_op jit(solution)/shard_map/all_to_all | solution.py:178
  123.4 10.1 %collective-permute-start.25 = (bf16[96,512]{1,0:T(8,128)(2,1)S(1)}, bf16[96,512]{1,0:T(8,128)(2,1)S(1)}, u32[]{:S(2)}, u32[]{:S(2)}) collective-permute-start(bf16[96,512]{1,0:T(8,128)(2,1)S(1)} %slice.265), channel_id=1, source_target_pairs={{0,128},{64,192},{128,0},{192,64},{256,384},{320,448},{384,256},{4... | collective-permute-start | bytes 294920 | tf_op jit(solution)/shard_map/ppermute | solution.py:155
  133.5 9.0 %collective-permute-start.26 = (bf16[32,512]{1,0:T(8,128)(2,1)S(1)}, bf16[32,512]{1,0:T(8,128)(2,1)S(1)}, u32[]{:S(2)}, u32[]{:S(2)}) collective-permute-start(bf16[32,512]{1,0:T(8,128)(2,1)S(1)} %slice.220), channel_id=1, source_target_pairs={{0,63},{1,2},{2,1},{3,4},{4,3},{5,6},{6,5},{7,8},{8,7},{9,10},{10,... | collective-permute-start | bytes 98312 | tf_op jit(solution)/shard_map/ppermute | solution.py:188
  136.8 9.4 %collective-permute-start.27 = (bf16[48,512]{1,0:T(8,128)(2,1)S(1)}, bf16[48,512]{1,0:T(8,128)(2,1)S(1)}, u32[]{:S(2)}, u32[]{:S(2)}) collective-permute-start(bf16[48,512]{1,0:T(8,128)(2,1)S(1)} %slice.268), channel_id=1, source_target_pairs={{0,256},{64,320},{128,384},{192,448},{256,0},{320,64},{384,128},{4... | collective-permute-start | bytes 147464 | tf_op jit(solution)/shard_map/ppermute | solution.py:155
  138.7 13.1 %all-to-all-start.1 = ((bf16[8,8,1152]{2,1,0:T(8,128)(2,1)}), bf16[8,8,1152]{2,1,0:T(8,128)(2,1)S(1)}, u32[]{:S(2)}, u32[]{:S(2)}) async-start(bf16[8,8,1152]{2,1,0:T(8,128)(2,1)} %bitcast.13), calls=%async_computation.1 | async-start | bytes 294912 | tf_op jit(solution)/shard_map/all_to_all | solution.py:185
  (32 other events, 225.4 us)

commit v3 on v2

--- a/solution.py
+++ b/solution.py
@@ -73,17 +73,18 @@
     label = jnp.arange(rows, dtype=jnp.int32)
     label = jnp.where(even & (label >= nodes), nodes + (label - nodes + rim) % (2 * rim), label)
 
-    picks = jnp.concatenate([halo_rows, jnp.arange(nodes, dtype=jnp.int32)])
-    chosen = lax.optimization_barrier(dot(onehot(picks, nodes), h).astype(bf16))
+    chosen = dot(onehot(halo_rows, nodes), h).astype(bf16)
     from_far = lax.ppermute(jnp.where(even, chosen[:rim], chosen[rim : 2 * rim]), "dom", far_pairs)
     from_near = lax.ppermute(jnp.where(even, chosen[rim : 2 * rim], chosen[:rim]), "dom", near_pairs)
     h_rim = jnp.concatenate([from_near, from_far], axis=0)
+    ends = lax.optimization_barrier(jnp.minimum(jnp.concatenate([edge_sender, edge_receiver]), rows - 1))
+    edge_sender, edge_receiver = ends[:edges], ends[edges:]
     send_hot = (edge_sender[:, None] == label[None, :]).astype(bf16)
     send_hot_t = (label[:, None] == edge_sender[None, :]).astype(bf16)
     recv_hot = onehot(edge_receiver, nodes)
     recv_hot_t = onehot_t(edge_receiver, nodes)
     live = (jnp.arange(edges, dtype=jnp.int32) // EDGE_BLOCK < block_counts[0]).astype(f32)[:, None]
-    own = dot(chosen[2 * rim :], w_send).astype(bf16)
+    own = dot(h, w_send).astype(bf16)
     base = lax.optimization_barrier(dot(feats, w_edge) + dot(send_hot[:, :nodes], own))
     pre = lax.optimization_barrier(base + dot(send_hot[:, nodes:], dot(h_rim, w_send).astype(bf16)))
     sig = jax.nn.sigmoid(pre)
@@ -109,10 +110,8 @@
         return dot_t(table[nodes:], w_send).astype(bf16)
 
     def joined(part, from_near, from_far):
-        (from_far,) = after(part, from_far)
-        total = lax.optimization_barrier(part.astype(f32) + dot(far_t, from_far))
-        (from_near,) = after(total, from_near)
-        return (total + dot(near_t, from_near)).astype(bf16)
+        rims = jnp.concatenate([from_near, from_far], axis=0)
+        return (part.astype(f32) + dot(select_t, rims)).astype(bf16)
 
     def hop(value, t, target):
         top = sections - 1 - t
@@ -123,28 +122,31 @@
     held = jnp.where(section == sections - 1, up, jnp.zeros_like(up))
     for t in range(sections - 1):
         _, table = backward(up)
-        rims = rim_part(table)
-        part = own_part(up, table)
+        back = dot_t(table, w_send)
+        part, rims = (up.astype(f32) + back[:nodes]).astype(bf16), back[nodes:].astype(bf16)
         if t == 0:
             (rows_late,) = after(part, halo_rows)
-            near_t = onehot_t(jnp.where(even, rows_late[rim:], rows_late[:rim]), nodes)
-            far_t = onehot_t(jnp.where(even, rows_late[:rim], rows_late[rim:]), nodes)
+            rows_late = jnp.where(even, jnp.concatenate([rows_late[rim:], rows_late[:rim]]), rows_late)
+            select_t = onehot_t(rows_late, nodes)
+        else:
+            held_late, up_late = after(part[:8, :128], held, up)
+            held = held_late + up_late
         from_far = hop(rims[rim:], t, far)
         from_near = hop(rims[:rim], t, near)
         up = joined(hop(part, t, range(doms)), from_near, from_far)
         if t == sections - 3:
-            feats_late, h_late, h_rim_late, dom_late, section_late = after(part, feats, h, h_rim, dom, section)
+            feats_late, h_late, h_rim_late, dom_late, section_late = after(
+                part[:8, :128], feats, h, h_rim, dom, section
+            )
             place = jnp.arange(doms, dtype=jnp.int32)
             chunk = (place % 8) * 8 + (place // 8 % 4) * 2 + (dom_late + place // 32) % 2
-            mixer = onehot(spread(chunk, width // doms), width)
+            order = spread(chunk, width // doms)
+            mixer = onehot(order, width)
             feats_t = dot_t(mixer, feats_late).astype(bf16)
             h_t = jnp.concatenate([dot_t(mixer, h_late), dot_t(mixer, h_rim_late)], axis=1).astype(bf16)
             s_order = lax.dynamic_index_in_dim(jnp.asarray(section_order(sections)), section_late, 0, keepdims=False)
             s_order = spread(s_order, edges // sections)
-            up, mixer, feats_t, h_t, s_order = lax.optimization_barrier((up, mixer, feats_t, h_t, s_order))
-        if t < sections - 2:
-            held = held + up
-            held, up = lax.optimization_barrier((held, up))
+            up, order, feats_t, h_t, s_order = lax.optimization_barrier((up, order, feats_t, h_t, s_order))
 
     up = held + up
     dpre, table = backward(up)
@@ -155,42 +157,44 @@
         return lax.ppermute(term[term.shape[0] // 2 :], "section", pairs)
 
     def section_add(term, got):
-        return (term[: term.shape[0] // 2].astype(f32) + got.astype(f32)).astype(bf16)
+        return (term[: got.shape[0]].astype(f32) + got.astype(f32)).astype(bf16)
 
     half = width // 2
     gain_rows = jnp.broadcast_to(gain_part.astype(bf16)[None], (128, width))
 
     def gradients(at):
-        return jnp.concatenate([dot(feats_t[at], dpre), dot(h_t[at], table), dot_t(mixer[at], gain_rows)], axis=1)
+        return jnp.concatenate([dot(feats_t[at], dpre), dot(h_t[at], table), dot_t(onehot(order[at], width), gain_rows)], axis=1)
 
     rims = rim_part(table)
     beside = jnp.pad(rims[:rim], ((0, 0), (0, width + 128)))
     payload = jnp.concatenate([gradients(slice(half, width)).astype(bf16), beside], axis=0)
     got = lax.ppermute(payload, "dom", near_pairs)
     (dpre_late,) = after(payload, dpre)
-    term = dot_t(dot(onehot(s_order, edges), dpre_late).astype(bf16), w_edge).astype(bf16)
-    section_got = section_send(term, 0)
-    from_near = got[half:, :width]
+    at = edges // 2
+    term_away = dot_t(dot(onehot(s_order[at:], edges), dpre_late).astype(bf16), w_edge).astype(bf16)
+    section_got = lax.ppermute(term_away, "section", [(s, s ^ 1) for s in range(sections)])
     sums = gradients(slice(0, half)) + got[:half].astype(f32)
-    (sums,) = after(term, sums.astype(bf16))
-
-    term, section_got = after(sums, term, section_got)
+    (sums,) = after(term_away, sums.astype(bf16))
+
+    dpre_late, section_got, rims, table, up = after(sums, dpre, section_got, rims, table, up)
+    term = dot_t(dot(onehot(s_order[:at], edges), dpre_late).astype(bf16), w_edge).astype(bf16)
     sums = lax.all_to_all(sums.reshape(4, half // 4, -1), "dom", 0, 0, axis_index_groups=ALONG_X)
     term = section_add(term, section_got)
     section_got = section_send(term, 1)
+    from_far = lax.ppermute(rims[rim:], "dom", far_pairs)
     sums = jnp.sum(sums.astype(f32), axis=0).astype(bf16)
     (sums,) = after(term, sums)
 
-    term, section_got, rims, table, up = after(sums, term, section_got, rims, table, up)
+    term, section_got = after(sums, term, section_got)
     sums = lax.all_to_all(sums.reshape(8, half // 32, -1), "dom", 0, 0, axis_index_groups=ALONG_Z)
     term = section_add(term, section_got)
     section_got = section_send(term, 2)
-    from_far = lax.ppermute(rims[rim:], "dom", far_pairs)
-    part = own_part(up, table)
+    got, from_far, table, up = after(term, got, from_far, table, up)
+    node_grads = joined(own_part(up, table), got[half:, :width], from_far)
     (sums,) = after(term, sums)
     sums = jnp.sum(sums.astype(f32), axis=0)
 
-    node_grads = joined(part, from_near, from_far)
+    term, section_got = after(sums, term, section_got)
     edge_grad, send_grad, gain_grad = sums[:, :width], sums[:, width : 2 * width], sums[:, 2 * width]
     term = section_add(term, section_got)
 

time: 154 us -> 146 us (0.948)
  waiting for transfers between devices: 61.6 us -> 47.6 us
  starting transfers between devices: 47.2 us -> 55.7 us
  matrix products: 24.9 us -> 23.3 us
    ppermute x21, waiting for transfers between devices: 47.1 us -> 38.5 us  [hop(): return lax.ppermute(value, ('section', 'dom'), pairs)]
    dot_general x22 -> x16, matrix products: 11.1 us -> 7.93 us  [dot_t(): lax.dot_general(a, b, (((1,), (1,)), ((), ())), preferred_element_type=jn...]
    ppermute x1, starting transfers between devices: 8.79 us -> 11.5 us  [on_device(): lax.ppermute(jnp.where(even, chosen[rim:2 * rim], chosen[:rim]), 'dom', n...]
    ppermute x1, starting transfers between devices: 1.92 us -> 4.51 us  [on_device(): lax.ppermute(jnp.where(even, chosen[:rim], chosen[rim:2 * rim]), 'dom', f...]
    ppermute x1, starting transfers between devices: 3.85 us -> 6.23 us  [on_device(): got = lax.ppermute(payload, 'dom', near_pairs)]
    all_to_all x1, waiting for transfers between devices: 6.61 us -> 4.31 us  [on_device(): lax.all_to_all(sums.reshape(4, half // 4, -1), 'dom', 0, 0, axis_index_gr...]
    ppermute x3 -> x2, starting transfers between devices: 5.89 us -> 3.83 us  [section_send(): return lax.ppermute(term[term.shape[0] // 2:], 'section', pairs)]
    ppermute x0 -> x1, starting transfers between devices: none -> 1.92 us  [on_device(): lax.ppermute(term_away, 'section', [(s, s ^ 1) for s in range(sections)])]
  transfers between devices with their start and end apart: 30 -> 30, of which waited for: 7 -> 6; matrix products, arithmetic and copies ran while one was open for 14% -> 13% of each run, Pallas kernels for 0% -> 0%
where the time goes in v3:
time: 146 us; the launch traced here: 144 us
  starting transfers between devices  55.7 us (38%)
  waiting for transfers between devices  47.6 us (33%)
  matrix products  23.3 us (16%)
  other arithmetic  10.5 us (7%)
  local copies, waits for them, and re-layouts  4.97 us (3%)
  between operations  2.36 us (2%)
    ppermute x21, waiting for transfers between devices, hop(): return lax.ppermute(value, ('section', 'dom'), pairs)  38.5 us
    ppermute x21, starting transfers between devices, hop(): return lax.ppermute(value, ('section', 'dom'), pairs)  17.5 us
    dot_general x26, matrix products, dot(): return jnp.dot(a, b, preferred_element_type=jnp.float32)  15.4 us
    ppermute x1, starting transfers between devices, on_device(): lax.ppermute(jnp.where(even, chosen[rim:2 * rim], chosen[:rim]), 'dom', n...  11.5 us
    dot_general x16, matrix products, dot_t(): lax.dot_general(a, b, (((1,), (1,)), ((), ())), preferred_element_type=jn...  7.93 us
    ppermute x1, starting transfers between devices, on_device(): got = lax.ppermute(payload, 'dom', near_pairs)  6.23 us
    ppermute x1, starting transfers between devices, on_device(): lax.ppermute(jnp.where(even, chosen[:rim], chosen[rim:2 * rim]), 'dom', f...  4.51 us
    all_to_all x1, waiting for transfers between devices, on_device(): lax.all_to_all(sums.reshape(4, half // 4, -1), 'dom', 0, 0, axis_index_gr...  4.31 us
  transfers between devices with their start and end apart: 30, of which 6 were waited for; matrix products, arithmetic and copies ran while one was open for 13% of the time, Pallas kernels for 0%

profile of v3, /device:TPU:1, one launch (start us, length us, event | category | flops | bytes accessed | tf_op | source)
XLA Modules:
  0.0 144.4 jit_solution(2393200312135835582)
XLA Ops:
  0.7 1.2 convolution_convert_fusion.21
  1.9 4.5 %collective-permute-start.1 = (bf16[32,512]{1,0:T(8,128)(2,1)S(1)}, bf16[32,512]{1,0:T(8,128)(2,1)S(1)}, u32[]{:S(2)}, u32[]{:S(2)}) collective-permute-start(bf16[32,512]{1,0:T(8,128)(2,1)S(1)} %get-tuple-element.101), channel_id=1, source_target_pairs={{0,63},{1,2},{2,1},{3,4},{4,3},{5,6},{6,5},{7,8},{8,7},{9,10},{10,... | collective-permute-start | bytes 98312 | tf_op jit(solution)/shard_map/ppermute | solution.py:77
  6.4 11.5 %collective-permute-start = (bf16[32,512]{1,0:T(8,128)(2,1)S(1)}, bf16[32,512]{1,0:T(8,128)(2,1)S(1)}, u32[]{:S(2)}, u32[]{:S(2)}) collective-permute-start(bf16[32,512]{1,0:T(8,128)(2,1)S(1)} %get-tuple-element.102), channel_id=1, source_target_pairs={{0,1},{1,0},{2,3},{3,2},{4,5},{5,4},{6,7},{7,6},{8,9},{9,8},{10,11... | collective-permute-start | bytes 98312 | tf_op jit(solution)/shard_map/ppermute | solution.py:78
  19.5 1.5 %fusion.13 = f32[384,512]{1,0:T(8,128)S(1)} fusion(bf16[1,512,512]{2,1,0:T(8,128)(2,1)S(1)} %copy-done, pred[384,256]{1,0:T(32,128)(4,1)S(1)} %broadcast_compare_fusion, bf16[1,1,192,512]{3,2,1,0:T(8,128)(2,1)} %param.11), kind=kOutput, calls=%fused_computation.43 | convolution fusion | flops 176259072 | bytes 1605632 | tf_op jit(solution)/shard_map/dot_general | solution.py:35
  39.0 1.3 convolution_convert_fusion.6
  47.0 1.3 collective-permute-start.18
  48.2 1.3 collective-permute-start.19
  49.7 1.0 convolution_convert_fusion.20
  50.7 1.2 convolution_convert_fusion.15
  51.9 1.2 convolution_convert_fusion
  57.9 1.4 collective-permute-start.21
  59.4 1.3 collective-permute-start.22
  60.7 1.5 %collective-permute-start.20 = (bf16[192,512]{1,0:T(8,128)(2,1)S(1)}, bf16[192,512]{1,0:T(8,128)(2,1)S(1)}, u32[]{:S(2)}, u32[]{:S(2)}) collective-permute-start(bf16[192,512]{1,0:T(8,128)(2,1)S(1)} %fusion.98), channel_id=1, source_target_pairs={{64,0},{65,1},{66,2},{67,3},{68,4},{69,5},{70,6},{71,7},{72,8},{73... | collective-permute-start | bytes 589832 | tf_op jit(solution)/shard_map/ppermute | solution.py:119
  62.2 38.0 %collective-permute-done.21 = bf16[32,512]{1,0:T(8,128)(2,1)S(1)} collective-permute-done((bf16[32,512]{1,0:T(8,128)(2,1)S(1)}, bf16[32,512]{1,0:T(8,128)(2,1)S(1)}, u32[]{:S(2)}, u32[]{:S(2)}) %collective-permute-start.21) | collective-permute-done | bytes 32800 | tf_op jit(solution)/shard_map/ppermute | solution.py:119
  104.4 6.2 %collective-permute-start.23 = (bf16[288,1152]{1,0:T(8,128)(2,1)}, bf16[288,1152]{1,0:T(8,128)(2,1)}, u32[]{:S(2)}, u32[]{:S(2)}) collective-permute-start(bf16[288,1152]{1,0:T(8,128)(2,1)} %fusion.24), channel_id=1, source_target_pairs={{0,1},{1,0},{2,3},{3,2},{4,5},{5,4},{6,7},{7,6},{8,9},{9,8},{10,11... | collective-permute-start | bytes 1990664 | tf_op jit(solution)/shard_map/ppermute | solution.py:171
  111.1 1.9 %collective-permute-start.24 = (bf16[192,512]{1,0:T(8,128)(2,1)S(1)}, bf16[192,512]{1,0:T(8,128)(2,1)S(1)}, u32[]{:S(2)}, u32[]{:S(2)}) collective-permute-start(bf16[192,512]{1,0:T(8,128)(2,1)S(1)} %convolution_convert_fusion.13), channel_id=1, source_target_pairs={{0,64},{64,0},{128,192},{192,128},{256,320},{320,256},{384,448},{4... | collective-permute-start | bytes 589832 | tf_op jit(solution)/shard_map/ppermute | solution.py:175
  113.9 2.0 %fusion.9 = bf16[256,1152]{1,0:T(8,128)(2,1)} fusion(f32[256,128]{1,0:T(8,128)S(1)} %fusion.52, f32[256,512]{1,0:T(8,128)S(1)} %fusion.209, f32[256,512]{1,0:T(8,128)S(1)} %fusion.124, bf16[288,1152]{1,0:T(8,128)(2,1)} %collective-permute-done.23), kind=kLoop, calls=%fused_computation.33 | loop fusion | flops 1474560 | bytes 2359296 | tf_op jit(solution)/shard_map/convert_element_type | solution.py:177
  115.9 3.5 %all-to-all-start = ((bf16[4,64,1152]{2,1,0:T(8,128)(2,1)}), bf16[4,64,1152]{2,1,0:T(8,128)(2,1)S(1)}, u32[]{:S(2)}, u32[]{:S(2)}) async-start(bf16[4,64,1152]{2,1,0:T(8,128)(2,1)} %bitcast.10), calls=%async_computation | async-start | bytes 1179648 | tf_op jit(solution)/shard_map/all_to_all | solution.py:181
  120.1 1.9 %collective-permute-start.25 = (bf16[96,512]{1,0:T(8,128)(2,1)S(1)}, bf16[96,512]{1,0:T(8,128)(2,1)S(1)}, u32[]{:S(2)}, u32[]{:S(2)}) collective-permute-start(bf16[96,512]{1,0:T(8,128)(2,1)S(1)} %slice.269), channel_id=1, source_target_pairs={{0,128},{64,192},{128,0},{192,64},{256,384},{320,448},{384,256},{4... | collective-permute-start | bytes 294920 | tf_op jit(solution)/shard_map/ppermute | solution.py:157
  122.0 3.4 %collective-permute-start.26 = (bf16[32,512]{1,0:T(8,128)(2,1)S(1)}, bf16[32,512]{1,0:T(8,128)(2,1)S(1)}, u32[]{:S(2)}, u32[]{:S(2)}) collective-permute-start(bf16[32,512]{1,0:T(8,128)(2,1)S(1)} %slice.232), channel_id=1, source_target_pairs={{0,63},{1,2},{2,1},{3,4},{4,3},{5,6},{6,5},{7,8},{8,7},{9,10},{10,... | collective-permute-start | bytes 98312 | tf_op jit(solution)/shard_map/ppermute | solution.py:184
  125.4 4.3 %all-to-all-done = bf16[4,64,1152]{2,1,0:T(8,128)(2,1)S(1)} async-done(((bf16[4,64,1152]{2,1,0:T(8,128)(2,1)}), bf16[4,64,1152]{2,1,0:T(8,128)(2,1)S(1)}, u32[]{:S(2)}, u32[]{:S(2)}) %all-to-all-start) | async-done | bytes 589856 | tf_op jit(solution)/shard_map/all_to_all | solution.py:181
  130.5 3.4 %all-to-all-start.1 = ((bf16[8,8,1152]{2,1,0:T(8,128)(2,1)}), bf16[8,8,1152]{2,1,0:T(8,128)(2,1)S(1)}, u32[]{:S(2)}, u32[]{:S(2)}) async-start(bf16[8,8,1152]{2,1,0:T(8,128)(2,1)} %bitcast.12), calls=%async_computation.1 | async-start | bytes 294912 | tf_op jit(solution)/shard_map/all_to_all | solution.py:189
  134.7 1.9 %collective-permute-start.27 = (bf16[48,512]{1,0:T(8,128)(2,1)S(1)}, bf16[48,512]{1,0:T(8,128)(2,1)S(1)}, u32[]{:S(2)}, u32[]{:S(2)}) collective-permute-start(bf16[48,512]{1,0:T(8,128)(2,1)S(1)} %slice.270), channel_id=1, source_target_pairs={{0,256},{64,320},{128,384},{192,448},{256,0},{320,64},{384,128},{4... | collective-permute-start | bytes 147464 | tf_op jit(solution)/shard_map/ppermute | solution.py:157
  137.9 3.9 %all-to-all-done.1 = bf16[8,8,1152]{2,1,0:T(8,128)(2,1)S(1)} async-done(((bf16[8,8,1152]{2,1,0:T(8,128)(2,1)}), bf16[8,8,1152]{2,1,0:T(8,128)(2,1)S(1)}, u32[]{:S(2)}, u32[]{:S(2)}) %all-to-all-start.1) | async-done | bytes 147488 | tf_op jit(solution)/shard_map/all_to_all | solution.py:189
  (186 shorter events, 41.5 us)
Async XLA Ops:
  1.9 19.5 %collective-permute-start.1 = (bf16[32,512]{1,0:T(8,128)(2,1)S(1)}, bf16[32,512]{1,0:T(8,128)(2,1)S(1)}, u32[]{:S(2)}, u32[]{:S(2)}) collective-permute-start(bf16[32,512]{1,0:T(8,128)(2,1)S(1)} %get-tuple-element.101), channel_id=1, source_target_pairs={{0,63},{1,2},{2,1},{3,4},{4,3},{5,6},{6,5},{7,8},{8,7},{9,10},{10,... | collective-permute-start | bytes 98312 | tf_op jit(solution)/shard_map/ppermute | solution.py:77
  6.4 15.0 %collective-permute-start = (bf16[32,512]{1,0:T(8,128)(2,1)S(1)}, bf16[32,512]{1,0:T(8,128)(2,1)S(1)}, u32[]{:S(2)}, u32[]{:S(2)}) collective-permute-start(bf16[32,512]{1,0:T(8,128)(2,1)S(1)} %get-tuple-element.102), channel_id=1, source_target_pairs={{0,1},{1,0},{2,3},{3,2},{4,5},{5,4},{6,7},{7,6},{8,9},{9,8},{10,11... | collective-permute-start | bytes 98312 | tf_op jit(solution)/shard_map/ppermute | solution.py:78
  24.4 2.2 %collective-permute-start.2 = (bf16[192,512]{1,0:T(8,128)(2,1)S(1)}, bf16[192,512]{1,0:T(8,128)(2,1)S(1)}, u32[]{:S(2)}, u32[]{:S(2)}) collective-permute-start(bf16[192,512]{1,0:T(8,128)(2,1)S(1)} %fusion.100), channel_id=1, source_target_pairs={{448,384},{449,385},{450,386},{451,387},{452,388},{453,389},{454,3... | collective-permute-start | bytes 589832 | tf_op jit(solution)/shard_map/ppermute | solution.py:119
  25.1 1.5 %collective-permute-start.3 = (bf16[32,512]{1,0:T(8,128)(2,1)S(1)}, bf16[32,512]{1,0:T(8,128)(2,1)S(1)}, u32[]{:S(2)}, u32[]{:S(2)}) collective-permute-start(bf16[32,512]{1,0:T(8,128)(2,1)S(1)} %get-tuple-element.99), channel_id=1, source_target_pairs={{448,385},{449,384},{450,387},{451,386},{452,389},{453,388},{454,3... | collective-permute-start | bytes 98312 | tf_op jit(solution)/shard_map/ppermute | solution.py:119
  27.9 2.1 %collective-permute-start.5 = (bf16[192,512]{1,0:T(8,128)(2,1)S(1)}, bf16[192,512]{1,0:T(8,128)(2,1)S(1)}, u32[]{:S(2)}, u32[]{:S(2)}) collective-permute-start(bf16[192,512]{1,0:T(8,128)(2,1)S(1)} %fusion.93), channel_id=1, source_target_pairs={{384,320},{385,321},{386,322},{387,323},{388,324},{389,325},{390,3... | collective-permute-start | bytes 589832 | tf_op jit(solution)/shard_map/ppermute | solution.py:119
  28.6 1.3 collective-permute-start.6
  31.4 2.1 %collective-permute-start.8 = (bf16[192,512]{1,0:T(8,128)(2,1)S(1)}, bf16[192,512]{1,0:T(8,128)(2,1)S(1)}, u32[]{:S(2)}, u32[]{:S(2)}) collective-permute-start(bf16[192,512]{1,0:T(8,128)(2,1)S(1)} %fusion.94), channel_id=1, source_target_pairs={{320,256},{321,257},{322,258},{323,259},{324,260},{325,261},{326,2... | collective-permute-start | bytes 589832 | tf_op jit(solution)/shard_map/ppermute | solution.py:119
  32.1 1.3 collective-permute-start.9
  34.8 2.7 %collective-permute-start.11 = (bf16[192,512]{1,0:T(8,128)(2,1)S(1)}, bf16[192,512]{1,0:T(8,128)(2,1)S(1)}, u32[]{:S(2)}, u32[]{:S(2)}) collective-permute-start(bf16[192,512]{1,0:T(8,128)(2,1)S(1)} %fusion.95), channel_id=1, source_target_pairs={{256,192},{257,193},{258,194},{259,195},{260,196},{261,197},{262,1... | collective-permute-start | bytes 589832 | tf_op jit(solution)/shard_map/ppermute | solution.py:119
  40.7 2.3 %collective-permute-start.15 = (bf16[32,512]{1,0:T(8,128)(2,1)S(1)}, bf16[32,512]{1,0:T(8,128)(2,1)S(1)}, u32[]{:S(2)}, u32[]{:S(2)}) collective-permute-start(bf16[32,512]{1,0:T(8,128)(2,1)S(1)} %get-tuple-element.91), channel_id=1, source_target_pairs={{192,129},{193,128},{194,131},{195,130},{196,133},{197,132},{198,1... | collective-permute-start | bytes 98312 | tf_op jit(solution)/shard_map/ppermute | solution.py:119
  41.4 1.6 %collective-permute-start.16 = (bf16[32,512]{1,0:T(8,128)(2,1)S(1)}, bf16[32,512]{1,0:T(8,128)(2,1)S(1)}, u32[]{:S(2)}, u32[]{:S(2)}) collective-permute-start(bf16[32,512]{1,0:T(8,128)(2,1)S(1)} %get-tuple-element.92), channel_id=1, source_target_pairs={{192,191},{193,130},{194,129},{195,132},{196,131},{197,134},{198,1... | collective-permute-start | bytes 98312 | tf_op jit(solution)/shard_map/ppermute | solution.py:119
  45.5 10.1 %collective-permute-start.17 = (bf16[192,512]{1,0:T(8,128)(2,1)}, bf16[192,512]{1,0:T(8,128)(2,1)S(1)}, u32[]{:S(2)}, u32[]{:S(2)}) collective-permute-start(bf16[192,512]{1,0:T(8,128)(2,1)} %fusion.97), channel_id=1, source_target_pairs={{128,64},{129,65},{130,66},{131,67},{132,68},{133,69},{134,70},{13... | collective-permute-start | bytes 589832 | tf_op jit(solution)/shard_map/ppermute | solution.py:119
  47.0 8.7 %collective-permute-start.18 = (bf16[32,512]{1,0:T(8,128)(2,1)}, bf16[32,512]{1,0:T(8,128)(2,1)}, u32[]{:S(2)}, u32[]{:S(2)}) collective-permute-start(bf16[32,512]{1,0:T(8,128)(2,1)} %get-tuple-element.89), channel_id=1, source_target_pairs={{128,65},{129,64},{130,67},{131,66},{132,69},{133,68},{134,71},{13... | collective-permute-start | bytes 98312 | tf_op jit(solution)/shard_map/ppermute | solution.py:119
  48.2 7.4 %collective-permute-start.19 = (bf16[32,512]{1,0:T(8,128)(2,1)}, bf16[32,512]{1,0:T(8,128)(2,1)}, u32[]{:S(2)}, u32[]{:S(2)}) collective-permute-start(bf16[32,512]{1,0:T(8,128)(2,1)} %get-tuple-element.90), channel_id=1, source_target_pairs={{128,127},{129,66},{130,65},{131,68},{132,67},{133,70},{134,69},{1... | collective-permute-start | bytes 98312 | tf_op jit(solution)/shard_map/ppermute | solution.py:119
  57.9 42.2 %collective-permute-start.21 = (bf16[32,512]{1,0:T(8,128)(2,1)S(1)}, bf16[32,512]{1,0:T(8,128)(2,1)S(1)}, u32[]{:S(2)}, u32[]{:S(2)}) collective-permute-start(bf16[32,512]{1,0:T(8,128)(2,1)S(1)} %get-tuple-element.87), channel_id=1, source_target_pairs={{64,1},{65,0},{66,3},{67,2},{68,5},{69,4},{70,7},{71,6},{72,9},{73... | collective-permute-start | bytes 98312 | tf_op jit(solution)/shard_map/ppermute | solution.py:119
  59.4 40.8 %collective-permute-start.22 = (bf16[32,512]{1,0:T(8,128)(2,1)S(1)}, bf16[32,512]{1,0:T(8,128)(2,1)S(1)}, u32[]{:S(2)}, u32[]{:S(2)}) collective-permute-start(bf16[32,512]{1,0:T(8,128)(2,1)S(1)} %get-tuple-element.88), channel_id=1, source_target_pairs={{64,63},{65,2},{66,1},{67,4},{68,3},{69,6},{70,5},{71,8},{72,7},{7... | collective-permute-start | bytes 98312 | tf_op jit(solution)/shard_map/ppermute | solution.py:119
  60.7 40.0 %collective-permute-start.20 = (bf16[192,512]{1,0:T(8,128)(2,1)S(1)}, bf16[192,512]{1,0:T(8,128)(2,1)S(1)}, u32[]{:S(2)}, u32[]{:S(2)}) collective-permute-start(bf16[192,512]{1,0:T(8,128)(2,1)S(1)} %fusion.98), channel_id=1, source_target_pairs={{64,0},{65,1},{66,2},{67,3},{68,4},{69,5},{70,6},{71,7},{72,8},{73... | collective-permute-start | bytes 589832 | tf_op jit(solution)/shard_map/ppermute | solution.py:119
  104.4 9.5 %collective-permute-start.23 = (bf16[288,1152]{1,0:T(8,128)(2,1)}, bf16[288,1152]{1,0:T(8,128)(2,1)}, u32[]{:S(2)}, u32[]{:S(2)}) collective-permute-start(bf16[288,1152]{1,0:T(8,128)(2,1)} %fusion.24), channel_id=1, source_target_pairs={{0,1},{1,0},{2,3},{3,2},{4,5},{5,4},{6,7},{7,6},{8,9},{9,8},{10,11... | collective-permute-start | bytes 1990664 | tf_op jit(solution)/shard_map/ppermute | solution.py:171
  111.1 8.4 %collective-permute-start.24 = (bf16[192,512]{1,0:T(8,128)(2,1)S(1)}, bf16[192,512]{1,0:T(8,128)(2,1)S(1)}, u32[]{:S(2)}, u32[]{:S(2)}) collective-permute-start(bf16[192,512]{1,0:T(8,128)(2,1)S(1)} %convolution_convert_fusion.13), channel_id=1, source_target_pairs={{0,64},{64,0},{128,192},{192,128},{256,320},{320,256},{384,448},{4... | collective-permute-start | bytes 589832 | tf_op jit(solution)/shard_map/ppermute | solution.py:175
  115.9 13.8 %all-to-all-start = ((bf16[4,64,1152]{2,1,0:T(8,128)(2,1)}), bf16[4,64,1152]{2,1,0:T(8,128)(2,1)S(1)}, u32[]{:S(2)}, u32[]{:S(2)}) async-start(bf16[4,64,1152]{2,1,0:T(8,128)(2,1)} %bitcast.10), calls=%async_computation | async-start | bytes 1179648 | tf_op jit(solution)/shard_map/all_to_all | solution.py:181
  120.1 13.8 %collective-permute-start.25 = (bf16[96,512]{1,0:T(8,128)(2,1)S(1)}, bf16[96,512]{1,0:T(8,128)(2,1)S(1)}, u32[]{:S(2)}, u32[]{:S(2)}) collective-permute-start(bf16[96,512]{1,0:T(8,128)(2,1)S(1)} %slice.269), channel_id=1, source_target_pairs={{0,128},{64,192},{128,0},{192,64},{256,384},{320,448},{384,256},{4... | collective-permute-start | bytes 294920 | tf_op jit(solution)/shard_map/ppermute | solution.py:157
  122.0 11.9 %collective-permute-start.26 = (bf16[32,512]{1,0:T(8,128)(2,1)S(1)}, bf16[32,512]{1,0:T(8,128)(2,1)S(1)}, u32[]{:S(2)}, u32[]{:S(2)}) collective-permute-start(bf16[32,512]{1,0:T(8,128)(2,1)S(1)} %slice.232), channel_id=1, source_target_pairs={{0,63},{1,2},{2,1},{3,4},{4,3},{5,6},{6,5},{7,8},{8,7},{9,10},{10,... | collective-permute-start | bytes 98312 | tf_op jit(solution)/shard_map/ppermute | solution.py:184
  130.5 11.2 %all-to-all-start.1 = ((bf16[8,8,1152]{2,1,0:T(8,128)(2,1)}), bf16[8,8,1152]{2,1,0:T(8,128)(2,1)S(1)}, u32[]{:S(2)}, u32[]{:S(2)}) async-start(bf16[8,8,1152]{2,1,0:T(8,128)(2,1)} %bitcast.12), calls=%async_computation.1 | async-start | bytes 294912 | tf_op jit(solution)/shard_map/all_to_all | solution.py:189
  134.7 9.0 %collective-permute-start.27 = (bf16[48,512]{1,0:T(8,128)(2,1)S(1)}, bf16[48,512]{1,0:T(8,128)(2,1)S(1)}, u32[]{:S(2)}, u32[]{:S(2)}) collective-permute-start(bf16[48,512]{1,0:T(8,128)(2,1)S(1)} %slice.270), channel_id=1, source_target_pairs={{0,256},{64,320},{128,384},{192,448},{256,0},{320,64},{384,128},{4... | collective-permute-start | bytes 147464 | tf_op jit(solution)/shard_map/ppermute | solution.py:157
  (28 other events, 180.4 us)

commit v4 on v3

--- a/solution.py
+++ b/solution.py
@@ -128,9 +128,16 @@
             (rows_late,) = after(part, halo_rows)
             rows_late = jnp.where(even, jnp.concatenate([rows_late[rim:], rows_late[:rim]]), rows_late)
             select_t = onehot_t(rows_late, nodes)
-        else:
+        elif t == 1:
             held_late, up_late = after(part[:8, :128], held, up)
             held = held_late + up_late
+        elif t % 2:
+            held_late, before_late, up_late = after(part[:8, :128], held, before, up)
+            held = held_late + (before_late + up_late)
+        elif t == sections - 2:
+            held_late, up_late = after(part[:8, :128], held, up)
+            held = held_late + up_late
+        before = up
         from_far = hop(rims[rim:], t, far)
         from_near = hop(rims[:rim], t, near)
         up = joined(hop(part, t, range(doms)), from_near, from_far)

time: 146 us -> 145 us (level)
  other arithmetic: 10.5 us -> 8.1 us
  waiting for transfers between devices: 47.6 us -> 49.7 us
    ppermute x21, waiting for transfers between devices: 38.5 us -> 40.6 us  [hop(): return lax.ppermute(value, ('section', 'dom'), pairs)]
  transfers between devices with their start and end apart: 30 -> 30, of which waited for: 6 -> 5; matrix products, arithmetic and copies ran while one was open for 13% -> 11% of each run, Pallas kernels for 0% -> 0%
where the time goes in v4:
time: 145 us; the launch traced here: 143 us
  starting transfers between devices  56.7 us (39%)
  waiting for transfers between devices  49.7 us (34%)
  matrix products  22.2 us (15%)
  other arithmetic  8.1 us (6%)
  local copies, waits for them, and re-layouts  4.21 us (3%)
  between operations  2.33 us (2%)
    ppermute x21, waiting for transfers between devices, hop(): return lax.ppermute(value, ('section', 'dom'), pairs)  40.6 us
    ppermute x21, starting transfers between devices, hop(): return lax.ppermute(value, ('section', 'dom'), pairs)  18.1 us
    dot_general x26, matrix products, dot(): return jnp.dot(a, b, preferred_element_type=jnp.float32)  14.2 us
    ppermute x1, starting transfers between devices, on_device(): lax.ppermute(jnp.where(even, chosen[rim:2 * rim], chosen[:rim]), 'dom', n...  11.5 us
    dot_general x16, matrix products, dot_t(): lax.dot_general(a, b, (((1,), (1,)), ((), ())), preferred_element_type=jn...  7.96 us
    ppermute x1, starting transfers between devices, on_device(): got = lax.ppermute(payload, 'dom', near_pairs)  6.69 us
    ppermute x1, starting transfers between devices, on_device(): lax.ppermute(jnp.where(even, chosen[:rim], chosen[rim:2 * rim]), 'dom', f...  4.51 us
    all_to_all x1, waiting for transfers between devices, on_device(): lax.all_to_all(sums.reshape(4, half // 4, -1), 'dom', 0, 0, axis_index_gr...  4.32 us
  transfers between devices with their start and end apart: 30, of which 5 were waited for; matrix products, arithmetic and copies ran while one was open for 11% of the time, Pallas kernels for 0%

profile of v4, /device:TPU:1, one launch (start us, length us, event | category | flops | bytes accessed | tf_op | source)
XLA Modules:
  0.0 143.2 jit_solution(7110988038792016064)
XLA Ops:
  0.7 1.2 convolution_convert_fusion.21
  1.9 4.5 %collective-permute-start.1 = (bf16[32,512]{1,0:T(8,128)(2,1)S(1)}, bf16[32,512]{1,0:T(8,128)(2,1)S(1)}, u32[]{:S(2)}, u32[]{:S(2)}) collective-permute-start(bf16[32,512]{1,0:T(8,128)(2,1)S(1)} %get-tuple-element.97), channel_id=1, source_target_pairs={{0,63},{1,2},{2,1},{3,4},{4,3},{5,6},{6,5},{7,8},{8,7},{9,10},{10,... | collective-permute-start | bytes 98312 | tf_op jit(solution)/shard_map/ppermute | solution.py:77
  6.4 11.5 %collective-permute-start = (bf16[32,512]{1,0:T(8,128)(2,1)S(1)}, bf16[32,512]{1,0:T(8,128)(2,1)S(1)}, u32[]{:S(2)}, u32[]{:S(2)}) collective-permute-start(bf16[32,512]{1,0:T(8,128)(2,1)S(1)} %get-tuple-element.98), channel_id=1, source_target_pairs={{0,1},{1,0},{2,3},{3,2},{4,5},{5,4},{6,7},{7,6},{8,9},{9,8},{10,11... | collective-permute-start | bytes 98312 | tf_op jit(solution)/shard_map/ppermute | solution.py:78
  19.5 1.5 %fusion.13 = f32[384,512]{1,0:T(8,128)S(1)} fusion(bf16[1,512,512]{2,1,0:T(8,128)(2,1)S(1)} %copy-done, pred[384,256]{1,0:T(32,128)(4,1)S(1)} %broadcast_compare_fusion, bf16[1,1,192,512]{3,2,1,0:T(8,128)(2,1)} %param.11), kind=kOutput, calls=%fused_computation.43 | convolution fusion | flops 176259072 | bytes 1605632 | tf_op jit(solution)/shard_map/dot_general | solution.py:35
  42.8 1.5 %collective-permute-start.17 = (bf16[192,512]{1,0:T(8,128)(2,1)}, bf16[192,512]{1,0:T(8,128)(2,1)}, u32[]{:S(2)}, u32[]{:S(2)}) collective-permute-start(bf16[192,512]{1,0:T(8,128)(2,1)} %fusion.97), channel_id=1, source_target_pairs={{128,64},{129,65},{130,66},{131,67},{132,68},{133,69},{134,70},{13... | collective-permute-start | bytes 589832 | tf_op jit(solution)/shard_map/ppermute | solution.py:119
  44.9 1.3 collective-permute-start.18
  46.1 1.3 collective-permute-start.19
  48.6 1.2 convolution_convert_fusion.15
  49.8 1.2 convolution_convert_fusion
  52.0 1.2 add_convert_fusion.2
  54.4 1.3 collective-permute-start.21
  55.7 1.3 collective-permute-start.22
  57.1 1.5 %collective-permute-start.20 = (bf16[192,512]{1,0:T(8,128)(2,1)S(1)}, bf16[192,512]{1,0:T(8,128)(2,1)S(1)}, u32[]{:S(2)}, u32[]{:S(2)}) collective-permute-start(bf16[192,512]{1,0:T(8,128)(2,1)S(1)} %fusion.98), channel_id=1, source_target_pairs={{64,0},{65,1},{66,2},{67,3},{68,4},{69,5},{70,6},{71,7},{72,8},{73... | collective-permute-start | bytes 589832 | tf_op jit(solution)/shard_map/ppermute | solution.py:119
  58.6 40.5 %collective-permute-done.21 = bf16[32,512]{1,0:T(8,128)(2,1)S(1)} collective-permute-done((bf16[32,512]{1,0:T(8,128)(2,1)S(1)}, bf16[32,512]{1,0:T(8,128)(2,1)S(1)}, u32[]{:S(2)}, u32[]{:S(2)}) %collective-permute-start.21) | collective-permute-done | bytes 32800 | tf_op jit(solution)/shard_map/ppermute | solution.py:119
  102.7 6.7 %collective-permute-start.23 = (bf16[288,1152]{1,0:T(8,128)(2,1)}, bf16[288,1152]{1,0:T(8,128)(2,1)}, u32[]{:S(2)}, u32[]{:S(2)}) collective-permute-start(bf16[288,1152]{1,0:T(8,128)(2,1)} %fusion.24), channel_id=1, source_target_pairs={{0,1},{1,0},{2,3},{3,2},{4,5},{5,4},{6,7},{7,6},{8,9},{9,8},{10,11... | collective-permute-start | bytes 1990664 | tf_op jit(solution)/shard_map/ppermute | solution.py:178
  109.9 1.9 %collective-permute-start.24 = (bf16[192,512]{1,0:T(8,128)(2,1)S(1)}, bf16[192,512]{1,0:T(8,128)(2,1)S(1)}, u32[]{:S(2)}, u32[]{:S(2)}) collective-permute-start(bf16[192,512]{1,0:T(8,128)(2,1)S(1)} %convolution_convert_fusion.13), channel_id=1, source_target_pairs={{0,64},{64,0},{128,192},{192,128},{256,320},{320,256},{384,448},{4... | collective-permute-start | bytes 589832 | tf_op jit(solution)/shard_map/ppermute | solution.py:182
  112.7 2.0 %fusion.9 = bf16[256,1152]{1,0:T(8,128)(2,1)} fusion(f32[256,128]{1,0:T(8,128)S(1)} %fusion.52, f32[256,512]{1,0:T(8,128)S(1)} %fusion.209, f32[256,512]{1,0:T(8,128)S(1)} %fusion.124, bf16[288,1152]{1,0:T(8,128)(2,1)} %collective-permute-done.23), kind=kLoop, calls=%fused_computation.33 | loop fusion | flops 1474560 | bytes 2359296 | tf_op jit(solution)/shard_map/convert_element_type | solution.py:184
  114.8 3.5 %all-to-all-start = ((bf16[4,64,1152]{2,1,0:T(8,128)(2,1)}), bf16[4,64,1152]{2,1,0:T(8,128)(2,1)S(1)}, u32[]{:S(2)}, u32[]{:S(2)}) async-start(bf16[4,64,1152]{2,1,0:T(8,128)(2,1)} %bitcast.10), calls=%async_computation | async-start | bytes 1179648 | tf_op jit(solution)/shard_map/all_to_all | solution.py:188
  118.9 1.9 %collective-permute-start.25 = (bf16[96,512]{1,0:T(8,128)(2,1)S(1)}, bf16[96,512]{1,0:T(8,128)(2,1)S(1)}, u32[]{:S(2)}, u32[]{:S(2)}) collective-permute-start(bf16[96,512]{1,0:T(8,128)(2,1)S(1)} %slice.267), channel_id=1, source_target_pairs={{0,128},{64,192},{128,0},{192,64},{256,384},{320,448},{384,256},{4... | collective-permute-start | bytes 294920 | tf_op jit(solution)/shard_map/ppermute | solution.py:164
  120.8 3.4 %collective-permute-start.26 = (bf16[32,512]{1,0:T(8,128)(2,1)S(1)}, bf16[32,512]{1,0:T(8,128)(2,1)S(1)}, u32[]{:S(2)}, u32[]{:S(2)}) collective-permute-start(bf16[32,512]{1,0:T(8,128)(2,1)S(1)} %slice.230), channel_id=1, source_target_pairs={{0,63},{1,2},{2,1},{3,4},{4,3},{5,6},{6,5},{7,8},{8,7},{9,10},{10,... | collective-permute-start | bytes 98312 | tf_op jit(solution)/shard_map/ppermute | solution.py:191
  124.2 4.3 %all-to-all-done = bf16[4,64,1152]{2,1,0:T(8,128)(2,1)S(1)} async-done(((bf16[4,64,1152]{2,1,0:T(8,128)(2,1)}), bf16[4,64,1152]{2,1,0:T(8,128)(2,1)S(1)}, u32[]{:S(2)}, u32[]{:S(2)}) %all-to-all-start) | async-done | bytes 589856 | tf_op jit(solution)/shard_map/all_to_all | solution.py:188
  129.3 3.4 %all-to-all-start.1 = ((bf16[8,8,1152]{2,1,0:T(8,128)(2,1)}), bf16[8,8,1152]{2,1,0:T(8,128)(2,1)S(1)}, u32[]{:S(2)}, u32[]{:S(2)}) async-start(bf16[8,8,1152]{2,1,0:T(8,128)(2,1)} %bitcast.12), calls=%async_computation.1 | async-start | bytes 294912 | tf_op jit(solution)/shard_map/all_to_all | solution.py:196
  133.5 1.9 %collective-permute-start.27 = (bf16[48,512]{1,0:T(8,128)(2,1)S(1)}, bf16[48,512]{1,0:T(8,128)(2,1)S(1)}, u32[]{:S(2)}, u32[]{:S(2)}) collective-permute-start(bf16[48,512]{1,0:T(8,128)(2,1)S(1)} %slice.268), channel_id=1, source_target_pairs={{0,256},{64,320},{128,384},{192,448},{256,0},{320,64},{384,128},{4... | collective-permute-start | bytes 147464 | tf_op jit(solution)/shard_map/ppermute | solution.py:164
  136.7 3.8 %all-to-all-done.1 = bf16[8,8,1152]{2,1,0:T(8,128)(2,1)S(1)} async-done(((bf16[8,8,1152]{2,1,0:T(8,128)(2,1)}), bf16[8,8,1152]{2,1,0:T(8,128)(2,1)S(1)}, u32[]{:S(2)}, u32[]{:S(2)}) %all-to-all-start.1) | async-done | bytes 147488 | tf_op jit(solution)/shard_map/all_to_all | solution.py:196
  (176 shorter events, 37.1 us)
Async XLA Ops:
  1.9 19.5 %collective-permute-start.1 = (bf16[32,512]{1,0:T(8,128)(2,1)S(1)}, bf16[32,512]{1,0:T(8,128)(2,1)S(1)}, u32[]{:S(2)}, u32[]{:S(2)}) collective-permute-start(bf16[32,512]{1,0:T(8,128)(2,1)S(1)} %get-tuple-element.97), channel_id=1, source_target_pairs={{0,63},{1,2},{2,1},{3,4},{4,3},{5,6},{6,5},{7,8},{8,7},{9,10},{10,... | collective-permute-start | bytes 98312 | tf_op jit(solution)/shard_map/ppermute | solution.py:77
  6.4 15.0 %collective-permute-start = (bf16[32,512]{1,0:T(8,128)(2,1)S(1)}, bf16[32,512]{1,0:T(8,128)(2,1)S(1)}, u32[]{:S(2)}, u32[]{:S(2)}) collective-permute-start(bf16[32,512]{1,0:T(8,128)(2,1)S(1)} %get-tuple-element.98), channel_id=1, source_target_pairs={{0,1},{1,0},{2,3},{3,2},{4,5},{5,4},{6,7},{7,6},{8,9},{9,8},{10,11... | collective-permute-start | bytes 98312 | tf_op jit(solution)/shard_map/ppermute | solution.py:78
  24.4 2.2 %collective-permute-start.2 = (bf16[192,512]{1,0:T(8,128)(2,1)S(1)}, bf16[192,512]{1,0:T(8,128)(2,1)S(1)}, u32[]{:S(2)}, u32[]{:S(2)}) collective-permute-start(bf16[192,512]{1,0:T(8,128)(2,1)S(1)} %fusion.100), channel_id=1, source_target_pairs={{448,384},{449,385},{450,386},{451,387},{452,388},{453,389},{454,3... | collective-permute-start | bytes 589832 | tf_op jit(solution)/shard_map/ppermute | solution.py:119
  25.1 1.5 %collective-permute-start.3 = (bf16[32,512]{1,0:T(8,128)(2,1)S(1)}, bf16[32,512]{1,0:T(8,128)(2,1)S(1)}, u32[]{:S(2)}, u32[]{:S(2)}) collective-permute-start(bf16[32,512]{1,0:T(8,128)(2,1)S(1)} %get-tuple-element.95), channel_id=1, source_target_pairs={{448,385},{449,384},{450,387},{451,386},{452,389},{453,388},{454,3... | collective-permute-start | bytes 98312 | tf_op jit(solution)/shard_map/ppermute | solution.py:119
  27.9 2.1 %collective-permute-start.5 = (bf16[192,512]{1,0:T(8,128)(2,1)S(1)}, bf16[192,512]{1,0:T(8,128)(2,1)S(1)}, u32[]{:S(2)}, u32[]{:S(2)}) collective-permute-start(bf16[192,512]{1,0:T(8,128)(2,1)S(1)} %fusion.93), channel_id=1, source_target_pairs={{384,320},{385,321},{386,322},{387,323},{388,324},{389,325},{390,3... | collective-permute-start | bytes 589832 | tf_op jit(solution)/shard_map/ppermute | solution.py:119
  31.4 2.1 %collective-permute-start.8 = (bf16[192,512]{1,0:T(8,128)(2,1)S(1)}, bf16[192,512]{1,0:T(8,128)(2,1)S(1)}, u32[]{:S(2)}, u32[]{:S(2)}) collective-permute-start(bf16[192,512]{1,0:T(8,128)(2,1)S(1)} %fusion.94), channel_id=1, source_target_pairs={{320,256},{321,257},{322,258},{323,259},{324,260},{325,261},{326,2... | collective-permute-start | bytes 589832 | tf_op jit(solution)/shard_map/ppermute | solution.py:119
  32.1 1.4 collective-permute-start.9
  34.8 2.1 %collective-permute-start.12 = (bf16[32,512]{1,0:T(8,128)(2,1)S(1)}, bf16[32,512]{1,0:T(8,128)(2,1)S(1)}, u32[]{:S(2)}, u32[]{:S(2)}) collective-permute-start(bf16[32,512]{1,0:T(8,128)(2,1)S(1)} %get-tuple-element.89), channel_id=1, source_target_pairs={{256,193},{257,192},{258,195},{259,194},{260,197},{261,196},{262,1... | collective-permute-start | bytes 98312 | tf_op jit(solution)/shard_map/ppermute | solution.py:119
  35.5 1.5 %collective-permute-start.13 = (bf16[32,512]{1,0:T(8,128)(2,1)S(1)}, bf16[32,512]{1,0:T(8,128)(2,1)S(1)}, u32[]{:S(2)}, u32[]{:S(2)}) collective-permute-start(bf16[32,512]{1,0:T(8,128)(2,1)S(1)} %get-tuple-element.90), channel_id=1, source_target_pairs={{256,255},{257,194},{258,193},{259,196},{260,195},{261,198},{262,1... | collective-permute-start | bytes 98312 | tf_op jit(solution)/shard_map/ppermute | solution.py:119
  38.6 2.1 %collective-permute-start.15 = (bf16[32,512]{1,0:T(8,128)(2,1)S(1)}, bf16[32,512]{1,0:T(8,128)(2,1)S(1)}, u32[]{:S(2)}, u32[]{:S(2)}) collective-permute-start(bf16[32,512]{1,0:T(8,128)(2,1)S(1)} %get-tuple-element.87), channel_id=1, source_target_pairs={{192,129},{193,128},{194,131},{195,130},{196,133},{197,132},{198,1... | collective-permute-start | bytes 98312 | tf_op jit(solution)/shard_map/ppermute | solution.py:119
  39.2 1.5 %collective-permute-start.16 = (bf16[32,512]{1,0:T(8,128)(2,1)S(1)}, bf16[32,512]{1,0:T(8,128)(2,1)S(1)}, u32[]{:S(2)}, u32[]{:S(2)}) collective-permute-start(bf16[32,512]{1,0:T(8,128)(2,1)S(1)} %get-tuple-element.88), channel_id=1, source_target_pairs={{192,191},{193,130},{194,129},{195,132},{196,131},{197,134},{198,1... | collective-permute-start | bytes 98312 | tf_op jit(solution)/shard_map/ppermute | solution.py:119
  42.8 9.2 %collective-permute-start.17 = (bf16[192,512]{1,0:T(8,128)(2,1)}, bf16[192,512]{1,0:T(8,128)(2,1)}, u32[]{:S(2)}, u32[]{:S(2)}) collective-permute-start(bf16[192,512]{1,0:T(8,128)(2,1)} %fusion.97), channel_id=1, source_target_pairs={{128,64},{129,65},{130,66},{131,67},{132,68},{133,69},{134,70},{13... | collective-permute-start | bytes 589832 | tf_op jit(solution)/shard_map/ppermute | solution.py:119
  44.9 7.1 %collective-permute-start.18 = (bf16[32,512]{1,0:T(8,128)(2,1)}, bf16[32,512]{1,0:T(8,128)(2,1)}, u32[]{:S(2)}, u32[]{:S(2)}) collective-permute-start(bf16[32,512]{1,0:T(8,128)(2,1)} %get-tuple-element.85), channel_id=1, source_target_pairs={{128,65},{129,64},{130,67},{131,66},{132,69},{133,68},{134,71},{13... | collective-permute-start | bytes 98312 | tf_op jit(solution)/shard_map/ppermute | solution.py:119
  46.1 5.8 %collective-permute-start.19 = (bf16[32,512]{1,0:T(8,128)(2,1)}, bf16[32,512]{1,0:T(8,128)(2,1)}, u32[]{:S(2)}, u32[]{:S(2)}) collective-permute-start(bf16[32,512]{1,0:T(8,128)(2,1)} %get-tuple-element.86), channel_id=1, source_target_pairs={{128,127},{129,66},{130,65},{131,68},{132,67},{133,70},{134,69},{1... | collective-permute-start | bytes 98312 | tf_op jit(solution)/shard_map/ppermute | solution.py:119
  54.4 44.7 %collective-permute-start.21 = (bf16[32,512]{1,0:T(8,128)(2,1)S(1)}, bf16[32,512]{1,0:T(8,128)(2,1)S(1)}, u32[]{:S(2)}, u32[]{:S(2)}) collective-permute-start(bf16[32,512]{1,0:T(8,128)(2,1)S(1)} %get-tuple-element.83), channel_id=1, source_target_pairs={{64,1},{65,0},{66,3},{67,2},{68,5},{69,4},{70,7},{71,6},{72,9},{73... | collective-permute-start | bytes 98312 | tf_op jit(solution)/shard_map/ppermute | solution.py:119
  55.7 43.4 %collective-permute-start.22 = (bf16[32,512]{1,0:T(8,128)(2,1)S(1)}, bf16[32,512]{1,0:T(8,128)(2,1)S(1)}, u32[]{:S(2)}, u32[]{:S(2)}) collective-permute-start(bf16[32,512]{1,0:T(8,128)(2,1)S(1)} %get-tuple-element.84), channel_id=1, source_target_pairs={{64,63},{65,2},{66,1},{67,4},{68,3},{69,6},{70,5},{71,8},{72,7},{7... | collective-permute-start | bytes 98312 | tf_op jit(solution)/shard_map/ppermute | solution.py:119
  57.1 42.0 %collective-permute-start.20 = (bf16[192,512]{1,0:T(8,128)(2,1)S(1)}, bf16[192,512]{1,0:T(8,128)(2,1)S(1)}, u32[]{:S(2)}, u32[]{:S(2)}) collective-permute-start(bf16[192,512]{1,0:T(8,128)(2,1)S(1)} %fusion.98), channel_id=1, source_target_pairs={{64,0},{65,1},{66,2},{67,3},{68,4},{69,5},{70,6},{71,7},{72,8},{73... | collective-permute-start | bytes 589832 | tf_op jit(solution)/shard_map/ppermute | solution.py:119
  102.7 10.0 %collective-permute-start.23 = (bf16[288,1152]{1,0:T(8,128)(2,1)}, bf16[288,1152]{1,0:T(8,128)(2,1)}, u32[]{:S(2)}, u32[]{:S(2)}) collective-permute-start(bf16[288,1152]{1,0:T(8,128)(2,1)} %fusion.24), channel_id=1, source_target_pairs={{0,1},{1,0},{2,3},{3,2},{4,5},{5,4},{6,7},{7,6},{8,9},{9,8},{10,11... | collective-permute-start | bytes 1990664 | tf_op jit(solution)/shard_map/ppermute | solution.py:178
  109.9 8.4 %collective-permute-start.24 = (bf16[192,512]{1,0:T(8,128)(2,1)S(1)}, bf16[192,512]{1,0:T(8,128)(2,1)S(1)}, u32[]{:S(2)}, u32[]{:S(2)}) collective-permute-start(bf16[192,512]{1,0:T(8,128)(2,1)S(1)} %convolution_convert_fusion.13), channel_id=1, source_target_pairs={{0,64},{64,0},{128,192},{192,128},{256,320},{320,256},{384,448},{4... | collective-permute-start | bytes 589832 | tf_op jit(solution)/shard_map/ppermute | solution.py:182
  114.8 13.8 %all-to-all-start = ((bf16[4,64,1152]{2,1,0:T(8,128)(2,1)}), bf16[4,64,1152]{2,1,0:T(8,128)(2,1)S(1)}, u32[]{:S(2)}, u32[]{:S(2)}) async-start(bf16[4,64,1152]{2,1,0:T(8,128)(2,1)} %bitcast.10), calls=%async_computation | async-start | bytes 1179648 | tf_op jit(solution)/shard_map/all_to_all | solution.py:188
  118.9 13.8 %collective-permute-start.25 = (bf16[96,512]{1,0:T(8,128)(2,1)S(1)}, bf16[96,512]{1,0:T(8,128)(2,1)S(1)}, u32[]{:S(2)}, u32[]{:S(2)}) collective-permute-start(bf16[96,512]{1,0:T(8,128)(2,1)S(1)} %slice.267), channel_id=1, source_target_pairs={{0,128},{64,192},{128,0},{192,64},{256,384},{320,448},{384,256},{4... | collective-permute-start | bytes 294920 | tf_op jit(solution)/shard_map/ppermute | solution.py:164
  120.8 11.9 %collective-permute-start.26 = (bf16[32,512]{1,0:T(8,128)(2,1)S(1)}, bf16[32,512]{1,0:T(8,128)(2,1)S(1)}, u32[]{:S(2)}, u32[]{:S(2)}) collective-permute-start(bf16[32,512]{1,0:T(8,128)(2,1)S(1)} %slice.230), channel_id=1, source_target_pairs={{0,63},{1,2},{2,1},{3,4},{4,3},{5,6},{6,5},{7,8},{8,7},{9,10},{10,... | collective-permute-start | bytes 98312 | tf_op jit(solution)/shard_map/ppermute | solution.py:191
  129.3 11.2 %all-to-all-start.1 = ((bf16[8,8,1152]{2,1,0:T(8,128)(2,1)}), bf16[8,8,1152]{2,1,0:T(8,128)(2,1)S(1)}, u32[]{:S(2)}, u32[]{:S(2)}) async-start(bf16[8,8,1152]{2,1,0:T(8,128)(2,1)} %bitcast.12), calls=%async_computation.1 | async-start | bytes 294912 | tf_op jit(solution)/shard_map/all_to_all | solution.py:196
  133.5 9.0 %collective-permute-start.27 = (bf16[48,512]{1,0:T(8,128)(2,1)S(1)}, bf16[48,512]{1,0:T(8,128)(2,1)S(1)}, u32[]{:S(2)}, u32[]{:S(2)}) collective-permute-start(bf16[48,512]{1,0:T(8,128)(2,1)S(1)} %slice.268), channel_id=1, source_target_pairs={{0,256},{64,320},{128,384},{192,448},{256,0},{320,64},{384,128},{4... | collective-permute-start | bytes 147464 | tf_op jit(solution)/shard_map/ppermute | solution.py:164
  (24 other events, 80.3 us)

commit v5 on v4

--- a/solution.py
+++ b/solution.py
@@ -77,6 +77,8 @@
     from_far = lax.ppermute(jnp.where(even, chosen[:rim], chosen[rim : 2 * rim]), "dom", far_pairs)
     from_near = lax.ppermute(jnp.where(even, chosen[rim : 2 * rim], chosen[:rim]), "dom", near_pairs)
     h_rim = jnp.concatenate([from_near, from_far], axis=0)
+    ends = lax.optimization_barrier(jnp.minimum(jnp.concatenate([edge_sender, edge_receiver]), rows - 1))
+    edge_sender, edge_receiver = ends[:edges], ends[edges:]
     ends = lax.optimization_barrier(jnp.minimum(jnp.concatenate([edge_sender, edge_receiver]), rows - 1))
     edge_sender, edge_receiver = ends[:edges], ends[edges:]
     send_hot = (edge_sender[:, None] == label[None, :]).astype(bf16)

time: 145 us -> 145 us (level)
  no operation moved by 1% of the time
where the time goes in v5:
time: 145 us; the launch traced here: 143 us
  starting transfers between devices  56.7 us (39%)
  waiting for transfers between devices  49.6 us (34%)
  matrix products  22.2 us (15%)
  other arithmetic  8.11 us (6%)
  local copies, waits for them, and re-layouts  4.21 us (3%)
  between operations  2.34 us (2%)
    ppermute x21, waiting for transfers between devices, hop(): return lax.ppermute(value, ('section', 'dom'), pairs)  40.6 us
    ppermute x21, starting transfers between devices, hop(): return lax.ppermute(value, ('section', 'dom'), pairs)  18.1 us
    dot_general x26, matrix products, dot(): return jnp.dot(a, b, preferred_element_type=jnp.float32)  14.2 us
    ppermute x1, starting transfers between devices, on_device(): lax.ppermute(jnp.where(even, chosen[rim:2 * rim], chosen[:rim]), 'dom', n...  11.5 us
    dot_general x16, matrix products, dot_t(): lax.dot_general(a, b, (((1,), (1,)), ((), ())), preferred_element_type=jn...  7.96 us
    ppermute x1, starting transfers between devices, on_device(): got = lax.ppermute(payload, 'dom', near_pairs)  6.69 us
    ppermute x1, starting transfers between devices, on_device(): lax.ppermute(jnp.where(even, chosen[:rim], chosen[rim:2 * rim]), 'dom', f...  4.51 us
    all_to_all x1, waiting for transfers between devices, on_device(): lax.all_to_all(sums.reshape(4, half // 4, -1), 'dom', 0, 0, axis_index_gr...  4.32 us
  transfers between devices with their start and end apart: 30, of which 5 were waited for; matrix products, arithmetic and copies ran while one was open for 11% of the time, Pallas kernels for 0%

profile of v5, /device:TPU:1, one launch (start us, length us, event | category | flops | bytes accessed | tf_op | source)
XLA Modules:
  0.0 143.2 jit_solution(15193608154171347432)
XLA Ops:
  0.7 1.2 convolution_convert_fusion.21
  1.9 4.5 %collective-permute-start.1 = (bf16[32,512]{1,0:T(8,128)(2,1)S(1)}, bf16[32,512]{1,0:T(8,128)(2,1)S(1)}, u32[]{:S(2)}, u32[]{:S(2)}) collective-permute-start(bf16[32,512]{1,0:T(8,128)(2,1)S(1)} %get-tuple-element.97), channel_id=1, source_target_pairs={{0,63},{1,2},{2,1},{3,4},{4,3},{5,6},{6,5},{7,8},{8,7},{9,10},{10,... | collective-permute-start | bytes 98312 | tf_op jit(solution)/shard_map/ppermute | solution.py:77
  6.4 11.5 %collective-permute-start = (bf16[32,512]{1,0:T(8,128)(2,1)S(1)}, bf16[32,512]{1,0:T(8,128)(2,1)S(1)}, u32[]{:S(2)}, u32[]{:S(2)}) collective-permute-start(bf16[32,512]{1,0:T(8,128)(2,1)S(1)} %get-tuple-element.98), channel_id=1, source_target_pairs={{0,1},{1,0},{2,3},{3,2},{4,5},{5,4},{6,7},{7,6},{8,9},{9,8},{10,11... | collective-permute-start | bytes 98312 | tf_op jit(solution)/shard_map/ppermute | solution.py:78
  19.5 1.5 %fusion.13 = f32[384,512]{1,0:T(8,128)S(1)} fusion(bf16[1,512,512]{2,1,0:T(8,128)(2,1)S(1)} %copy-done, pred[384,256]{1,0:T(32,128)(4,1)S(1)} %broadcast_compare_fusion, bf16[1,1,192,512]{3,2,1,0:T(8,128)(2,1)} %param.11), kind=kOutput, calls=%fused_computation.43 | convolution fusion | flops 176259072 | bytes 1605632 | tf_op jit(solution)/shard_map/dot_general | solution.py:35
  42.8 1.5 %collective-permute-start.17 = (bf16[192,512]{1,0:T(8,128)(2,1)}, bf16[192,512]{1,0:T(8,128)(2,1)}, u32[]{:S(2)}, u32[]{:S(2)}) collective-permute-start(bf16[192,512]{1,0:T(8,128)(2,1)} %fusion.97), channel_id=1, source_target_pairs={{128,64},{129,65},{130,66},{131,67},{132,68},{133,69},{134,70},{13... | collective-permute-start | bytes 589832 | tf_op jit(solution)/shard_map/ppermute | solution.py:121
  44.9 1.3 collective-permute-start.18
  46.2 1.3 collective-permute-start.19
  48.7 1.2 convolution_convert_fusion.15
  49.8 1.2 convolution_convert_fusion
  52.0 1.2 add_convert_fusion.2
  54.4 1.3 collective-permute-start.21
  55.7 1.3 collective-permute-start.22
  57.1 1.5 %collective-permute-start.20 = (bf16[192,512]{1,0:T(8,128)(2,1)S(1)}, bf16[192,512]{1,0:T(8,128)(2,1)S(1)}, u32[]{:S(2)}, u32[]{:S(2)}) collective-permute-start(bf16[192,512]{1,0:T(8,128)(2,1)S(1)} %fusion.98), channel_id=1, source_target_pairs={{64,0},{65,1},{66,2},{67,3},{68,4},{69,5},{70,6},{71,7},{72,8},{73... | collective-permute-start | bytes 589832 | tf_op jit(solution)/shard_map/ppermute | solution.py:121
  58.6 40.5 %collective-permute-done.21 = bf16[32,512]{1,0:T(8,128)(2,1)S(1)} collective-permute-done((bf16[32,512]{1,0:T(8,128)(2,1)S(1)}, bf16[32,512]{1,0:T(8,128)(2,1)S(1)}, u32[]{:S(2)}, u32[]{:S(2)}) %collective-permute-start.21) | collective-permute-done | bytes 32800 | tf_op jit(solution)/shard_map/ppermute | solution.py:121
  102.7 6.7 %collective-permute-start.23 = (bf16[288,1152]{1,0:T(8,128)(2,1)}, bf16[288,1152]{1,0:T(8,128)(2,1)}, u32[]{:S(2)}, u32[]{:S(2)}) collective-permute-start(bf16[288,1152]{1,0:T(8,128)(2,1)} %fusion.24), channel_id=1, source_target_pairs={{0,1},{1,0},{2,3},{3,2},{4,5},{5,4},{6,7},{7,6},{8,9},{9,8},{10,11... | collective-permute-start | bytes 1990664 | tf_op jit(solution)/shard_map/ppermute | solution.py:180
  109.9 1.9 %collective-permute-start.24 = (bf16[192,512]{1,0:T(8,128)(2,1)S(1)}, bf16[192,512]{1,0:T(8,128)(2,1)S(1)}, u32[]{:S(2)}, u32[]{:S(2)}) collective-permute-start(bf16[192,512]{1,0:T(8,128)(2,1)S(1)} %convolution_convert_fusion.13), channel_id=1, source_target_pairs={{0,64},{64,0},{128,192},{192,128},{256,320},{320,256},{384,448},{4... | collective-permute-start | bytes 589832 | tf_op jit(solution)/shard_map/ppermute | solution.py:184
  112.7 2.0 %fusion.9 = bf16[256,1152]{1,0:T(8,128)(2,1)} fusion(f32[256,128]{1,0:T(8,128)S(1)} %fusion.52, f32[256,512]{1,0:T(8,128)S(1)} %fusion.209, f32[256,512]{1,0:T(8,128)S(1)} %fusion.124, bf16[288,1152]{1,0:T(8,128)(2,1)} %collective-permute-done.23), kind=kLoop, calls=%fused_computation.33 | loop fusion | flops 1474560 | bytes 2359296 | tf_op jit(solution)/shard_map/convert_element_type | solution.py:186
  114.8 3.5 %all-to-all-start = ((bf16[4,64,1152]{2,1,0:T(8,128)(2,1)}), bf16[4,64,1152]{2,1,0:T(8,128)(2,1)S(1)}, u32[]{:S(2)}, u32[]{:S(2)}) async-start(bf16[4,64,1152]{2,1,0:T(8,128)(2,1)} %bitcast.10), calls=%async_computation | async-start | bytes 1179648 | tf_op jit(solution)/shard_map/all_to_all | solution.py:190
  118.9 1.9 %collective-permute-start.25 = (bf16[96,512]{1,0:T(8,128)(2,1)S(1)}, bf16[96,512]{1,0:T(8,128)(2,1)S(1)}, u32[]{:S(2)}, u32[]{:S(2)}) collective-permute-start(bf16[96,512]{1,0:T(8,128)(2,1)S(1)} %slice.270), channel_id=1, source_target_pairs={{0,128},{64,192},{128,0},{192,64},{256,384},{320,448},{384,256},{4... | collective-permute-start | bytes 294920 | tf_op jit(solution)/shard_map/ppermute | solution.py:166
  120.8 3.4 %collective-permute-start.26 = (bf16[32,512]{1,0:T(8,128)(2,1)S(1)}, bf16[32,512]{1,0:T(8,128)(2,1)S(1)}, u32[]{:S(2)}, u32[]{:S(2)}) collective-permute-start(bf16[32,512]{1,0:T(8,128)(2,1)S(1)} %slice.233), channel_id=1, source_target_pairs={{0,63},{1,2},{2,1},{3,4},{4,3},{5,6},{6,5},{7,8},{8,7},{9,10},{10,... | collective-permute-start | bytes 98312 | tf_op jit(solution)/shard_map/ppermute | solution.py:193
  124.2 4.3 %all-to-all-done = bf16[4,64,1152]{2,1,0:T(8,128)(2,1)S(1)} async-done(((bf16[4,64,1152]{2,1,0:T(8,128)(2,1)}), bf16[4,64,1152]{2,1,0:T(8,128)(2,1)S(1)}, u32[]{:S(2)}, u32[]{:S(2)}) %all-to-all-start) | async-done | bytes 589856 | tf_op jit(solution)/shard_map/all_to_all | solution.py:190
  129.3 3.4 %all-to-all-start.1 = ((bf16[8,8,1152]{2,1,0:T(8,128)(2,1)}), bf16[8,8,1152]{2,1,0:T(8,128)(2,1)S(1)}, u32[]{:S(2)}, u32[]{:S(2)}) async-start(bf16[8,8,1152]{2,1,0:T(8,128)(2,1)} %bitcast.12), calls=%async_computation.1 | async-start | bytes 294912 | tf_op jit(solution)/shard_map/all_to_all | solution.py:198
  133.5 1.9 %collective-permute-start.27 = (bf16[48,512]{1,0:T(8,128)(2,1)S(1)}, bf16[48,512]{1,0:T(8,128)(2,1)S(1)}, u32[]{:S(2)}, u32[]{:S(2)}) collective-permute-start(bf16[48,512]{1,0:T(8,128)(2,1)S(1)} %slice.271), channel_id=1, source_target_pairs={{0,256},{64,320},{128,384},{192,448},{256,0},{320,64},{384,128},{4... | collective-permute-start | bytes 147464 | tf_op jit(solution)/shard_map/ppermute | solution.py:166
  136.7 3.8 %all-to-all-done.1 = bf16[8,8,1152]{2,1,0:T(8,128)(2,1)S(1)} async-done(((bf16[8,8,1152]{2,1,0:T(8,128)(2,1)}), bf16[8,8,1152]{2,1,0:T(8,128)(2,1)S(1)}, u32[]{:S(2)}, u32[]{:S(2)}) %all-to-all-start.1) | async-done | bytes 147488 | tf_op jit(solution)/shard_map/all_to_all | solution.py:198
  (177 shorter events, 37.1 us)
Async XLA Ops:
  1.9 19.6 %collective-permute-start.1 = (bf16[32,512]{1,0:T(8,128)(2,1)S(1)}, bf16[32,512]{1,0:T(8,128)(2,1)S(1)}, u32[]{:S(2)}, u32[]{:S(2)}) collective-permute-start(bf16[32,512]{1,0:T(8,128)(2,1)S(1)} %get-tuple-element.97), channel_id=1, source_target_pairs={{0,63},{1,2},{2,1},{3,4},{4,3},{5,6},{6,5},{7,8},{8,7},{9,10},{10,... | collective-permute-start | bytes 98312 | tf_op jit(solution)/shard_map/ppermute | solution.py:77
  6.4 15.0 %collective-permute-start = (bf16[32,512]{1,0:T(8,128)(2,1)S(1)}, bf16[32,512]{1,0:T(8,128)(2,1)S(1)}, u32[]{:S(2)}, u32[]{:S(2)}) collective-permute-start(bf16[32,512]{1,0:T(8,128)(2,1)S(1)} %get-tuple-element.98), channel_id=1, source_target_pairs={{0,1},{1,0},{2,3},{3,2},{4,5},{5,4},{6,7},{7,6},{8,9},{9,8},{10,11... | collective-permute-start | bytes 98312 | tf_op jit(solution)/shard_map/ppermute | solution.py:78
  24.4 2.2 %collective-permute-start.2 = (bf16[192,512]{1,0:T(8,128)(2,1)S(1)}, bf16[192,512]{1,0:T(8,128)(2,1)S(1)}, u32[]{:S(2)}, u32[]{:S(2)}) collective-permute-start(bf16[192,512]{1,0:T(8,128)(2,1)S(1)} %fusion.100), channel_id=1, source_target_pairs={{448,384},{449,385},{450,386},{451,387},{452,388},{453,389},{454,3... | collective-permute-start | bytes 589832 | tf_op jit(solution)/shard_map/ppermute | solution.py:121
  25.1 1.5 %collective-permute-start.3 = (bf16[32,512]{1,0:T(8,128)(2,1)S(1)}, bf16[32,512]{1,0:T(8,128)(2,1)S(1)}, u32[]{:S(2)}, u32[]{:S(2)}) collective-permute-start(bf16[32,512]{1,0:T(8,128)(2,1)S(1)} %get-tuple-element.95), channel_id=1, source_target_pairs={{448,385},{449,384},{450,387},{451,386},{452,389},{453,388},{454,3... | collective-permute-start | bytes 98312 | tf_op jit(solution)/shard_map/ppermute | solution.py:121
  28.0 2.1 %collective-permute-start.5 = (bf16[192,512]{1,0:T(8,128)(2,1)S(1)}, bf16[192,512]{1,0:T(8,128)(2,1)S(1)}, u32[]{:S(2)}, u32[]{:S(2)}) collective-permute-start(bf16[192,512]{1,0:T(8,128)(2,1)S(1)} %fusion.93), channel_id=1, source_target_pairs={{384,320},{385,321},{386,322},{387,323},{388,324},{389,325},{390,3... | collective-permute-start | bytes 589832 | tf_op jit(solution)/shard_map/ppermute | solution.py:121
  31.4 2.1 %collective-permute-start.8 = (bf16[192,512]{1,0:T(8,128)(2,1)S(1)}, bf16[192,512]{1,0:T(8,128)(2,1)S(1)}, u32[]{:S(2)}, u32[]{:S(2)}) collective-permute-start(bf16[192,512]{1,0:T(8,128)(2,1)S(1)} %fusion.94), channel_id=1, source_target_pairs={{320,256},{321,257},{322,258},{323,259},{324,260},{325,261},{326,2... | collective-permute-start | bytes 589832 | tf_op jit(solution)/shard_map/ppermute | solution.py:121
  32.1 1.4 collective-permute-start.9
  34.8 2.1 %collective-permute-start.12 = (bf16[32,512]{1,0:T(8,128)(2,1)S(1)}, bf16[32,512]{1,0:T(8,128)(2,1)S(1)}, u32[]{:S(2)}, u32[]{:S(2)}) collective-permute-start(bf16[32,512]{1,0:T(8,128)(2,1)S(1)} %get-tuple-element.89), channel_id=1, source_target_pairs={{256,193},{257,192},{258,195},{259,194},{260,197},{261,196},{262,1... | collective-permute-start | bytes 98312 | tf_op jit(solution)/shard_map/ppermute | solution.py:121
  35.5 1.5 %collective-permute-start.13 = (bf16[32,512]{1,0:T(8,128)(2,1)S(1)}, bf16[32,512]{1,0:T(8,128)(2,1)S(1)}, u32[]{:S(2)}, u32[]{:S(2)}) collective-permute-start(bf16[32,512]{1,0:T(8,128)(2,1)S(1)} %get-tuple-element.90), channel_id=1, source_target_pairs={{256,255},{257,194},{258,193},{259,196},{260,195},{261,198},{262,1... | collective-permute-start | bytes 98312 | tf_op jit(solution)/shard_map/ppermute | solution.py:121
  38.6 2.1 %collective-permute-start.15 = (bf16[32,512]{1,0:T(8,128)(2,1)S(1)}, bf16[32,512]{1,0:T(8,128)(2,1)S(1)}, u32[]{:S(2)}, u32[]{:S(2)}) collective-permute-start(bf16[32,512]{1,0:T(8,128)(2,1)S(1)} %get-tuple-element.87), channel_id=1, source_target_pairs={{192,129},{193,128},{194,131},{195,130},{196,133},{197,132},{198,1... | collective-permute-start | bytes 98312 | tf_op jit(solution)/shard_map/ppermute | solution.py:121
  39.3 1.5 %collective-permute-start.16 = (bf16[32,512]{1,0:T(8,128)(2,1)S(1)}, bf16[32,512]{1,0:T(8,128)(2,1)S(1)}, u32[]{:S(2)}, u32[]{:S(2)}) collective-permute-start(bf16[32,512]{1,0:T(8,128)(2,1)S(1)} %get-tuple-element.88), channel_id=1, source_target_pairs={{192,191},{193,130},{194,129},{195,132},{196,131},{197,134},{198,1... | collective-permute-start | bytes 98312 | tf_op jit(solution)/shard_map/ppermute | solution.py:121
  42.8 9.2 %collective-permute-start.17 = (bf16[192,512]{1,0:T(8,128)(2,1)}, bf16[192,512]{1,0:T(8,128)(2,1)}, u32[]{:S(2)}, u32[]{:S(2)}) collective-permute-start(bf16[192,512]{1,0:T(8,128)(2,1)} %fusion.97), channel_id=1, source_target_pairs={{128,64},{129,65},{130,66},{131,67},{132,68},{133,69},{134,70},{13... | collective-permute-start | bytes 589832 | tf_op jit(solution)/shard_map/ppermute | solution.py:121
  44.9 7.1 %collective-permute-start.18 = (bf16[32,512]{1,0:T(8,128)(2,1)}, bf16[32,512]{1,0:T(8,128)(2,1)}, u32[]{:S(2)}, u32[]{:S(2)}) collective-permute-start(bf16[32,512]{1,0:T(8,128)(2,1)} %get-tuple-element.85), channel_id=1, source_target_pairs={{128,65},{129,64},{130,67},{131,66},{132,69},{133,68},{134,71},{13... | collective-permute-start | bytes 98312 | tf_op jit(solution)/shard_map/ppermute | solution.py:121
  46.2 5.8 %collective-permute-start.19 = (bf16[32,512]{1,0:T(8,128)(2,1)}, bf16[32,512]{1,0:T(8,128)(2,1)}, u32[]{:S(2)}, u32[]{:S(2)}) collective-permute-start(bf16[32,512]{1,0:T(8,128)(2,1)} %get-tuple-element.86), channel_id=1, source_target_pairs={{128,127},{129,66},{130,65},{131,68},{132,67},{133,70},{134,69},{1... | collective-permute-start | bytes 98312 | tf_op jit(solution)/shard_map/ppermute | solution.py:121
  54.4 44.7 %collective-permute-start.21 = (bf16[32,512]{1,0:T(8,128)(2,1)S(1)}, bf16[32,512]{1,0:T(8,128)(2,1)S(1)}, u32[]{:S(2)}, u32[]{:S(2)}) collective-permute-start(bf16[32,512]{1,0:T(8,128)(2,1)S(1)} %get-tuple-element.83), channel_id=1, source_target_pairs={{64,1},{65,0},{66,3},{67,2},{68,5},{69,4},{70,7},{71,6},{72,9},{73... | collective-permute-start | bytes 98312 | tf_op jit(solution)/shard_map/ppermute | solution.py:121
  55.7 43.4 %collective-permute-start.22 = (bf16[32,512]{1,0:T(8,128)(2,1)S(1)}, bf16[32,512]{1,0:T(8,128)(2,1)S(1)}, u32[]{:S(2)}, u32[]{:S(2)}) collective-permute-start(bf16[32,512]{1,0:T(8,128)(2,1)S(1)} %get-tuple-element.84), channel_id=1, source_target_pairs={{64,63},{65,2},{66,1},{67,4},{68,3},{69,6},{70,5},{71,8},{72,7},{7... | collective-permute-start | bytes 98312 | tf_op jit(solution)/shard_map/ppermute | solution.py:121
  57.1 42.0 %collective-permute-start.20 = (bf16[192,512]{1,0:T(8,128)(2,1)S(1)}, bf16[192,512]{1,0:T(8,128)(2,1)S(1)}, u32[]{:S(2)}, u32[]{:S(2)}) collective-permute-start(bf16[192,512]{1,0:T(8,128)(2,1)S(1)} %fusion.98), channel_id=1, source_target_pairs={{64,0},{65,1},{66,2},{67,3},{68,4},{69,5},{70,6},{71,7},{72,8},{73... | collective-permute-start | bytes 589832 | tf_op jit(solution)/shard_map/ppermute | solution.py:121
  102.7 10.0 %collective-permute-start.23 = (bf16[288,1152]{1,0:T(8,128)(2,1)}, bf16[288,1152]{1,0:T(8,128)(2,1)}, u32[]{:S(2)}, u32[]{:S(2)}) collective-permute-start(bf16[288,1152]{1,0:T(8,128)(2,1)} %fusion.24), channel_id=1, source_target_pairs={{0,1},{1,0},{2,3},{3,2},{4,5},{5,4},{6,7},{7,6},{8,9},{9,8},{10,11... | collective-permute-start | bytes 1990664 | tf_op jit(solution)/shard_map/ppermute | solution.py:180
  109.9 8.4 %collective-permute-start.24 = (bf16[192,512]{1,0:T(8,128)(2,1)S(1)}, bf16[192,512]{1,0:T(8,128)(2,1)S(1)}, u32[]{:S(2)}, u32[]{:S(2)}) collective-permute-start(bf16[192,512]{1,0:T(8,128)(2,1)S(1)} %convolution_convert_fusion.13), channel_id=1, source_target_pairs={{0,64},{64,0},{128,192},{192,128},{256,320},{320,256},{384,448},{4... | collective-permute-start | bytes 589832 | tf_op jit(solution)/shard_map/ppermute | solution.py:184
  114.8 13.8 %all-to-all-start = ((bf16[4,64,1152]{2,1,0:T(8,128)(2,1)}), bf16[4,64,1152]{2,1,0:T(8,128)(2,1)S(1)}, u32[]{:S(2)}, u32[]{:S(2)}) async-start(bf16[4,64,1152]{2,1,0:T(8,128)(2,1)} %bitcast.10), calls=%async_computation | async-start | bytes 1179648 | tf_op jit(solution)/shard_map/all_to_all | solution.py:190
  118.9 13.8 %collective-permute-start.25 = (bf16[96,512]{1,0:T(8,128)(2,1)S(1)}, bf16[96,512]{1,0:T(8,128)(2,1)S(1)}, u32[]{:S(2)}, u32[]{:S(2)}) collective-permute-start(bf16[96,512]{1,0:T(8,128)(2,1)S(1)} %slice.270), channel_id=1, source_target_pairs={{0,128},{64,192},{128,0},{192,64},{256,384},{320,448},{384,256},{4... | collective-permute-start | bytes 294920 | tf_op jit(solution)/shard_map/ppermute | solution.py:166
  120.8 11.9 %collective-permute-start.26 = (bf16[32,512]{1,0:T(8,128)(2,1)S(1)}, bf16[32,512]{1,0:T(8,128)(2,1)S(1)}, u32[]{:S(2)}, u32[]{:S(2)}) collective-permute-start(bf16[32,512]{1,0:T(8,128)(2,1)S(1)} %slice.233), channel_id=1, source_target_pairs={{0,63},{1,2},{2,1},{3,4},{4,3},{5,6},{6,5},{7,8},{8,7},{9,10},{10,... | collective-permute-start | bytes 98312 | tf_op jit(solution)/shard_map/ppermute | solution.py:193
  129.3 11.2 %all-to-all-start.1 = ((bf16[8,8,1152]{2,1,0:T(8,128)(2,1)}), bf16[8,8,1152]{2,1,0:T(8,128)(2,1)S(1)}, u32[]{:S(2)}, u32[]{:S(2)}) async-start(bf16[8,8,1152]{2,1,0:T(8,128)(2,1)} %bitcast.12), calls=%async_computation.1 | async-start | bytes 294912 | tf_op jit(solution)/shard_map/all_to_all | solution.py:198
  133.5 9.0 %collective-permute-start.27 = (bf16[48,512]{1,0:T(8,128)(2,1)S(1)}, bf16[48,512]{1,0:T(8,128)(2,1)S(1)}, u32[]{:S(2)}, u32[]{:S(2)}) collective-permute-start(bf16[48,512]{1,0:T(8,128)(2,1)S(1)} %slice.271), channel_id=1, source_target_pairs={{0,256},{64,320},{128,384},{192,448},{256,0},{320,64},{384,128},{4... | collective-permute-start | bytes 147464 | tf_op jit(solution)/shard_map/ppermute | solution.py:166
  (24 other events, 80.3 us)
